TPU v7x, 256 devices: a whole 4x4x8 slice. The times are simulated.
256 devices in a mesh: wide: 16 (over y, x), narrow: 16 (over z, core).
Axes of the slice: x: 4, y: 4, z: 8, core: 2. Of those that a mesh axis runs over, the one named last changes fastest.
Arguments:
- positions: float32 [3072, 3, 256], P(('wide', 'narrow')), may hold values from 6 to 18
- forces: float32 [3072, 256], P(('wide', 'narrow')), may hold values from -0.6 to 0.6
- counts: int32 [3072], P(('wide', 'narrow')), may hold values from 0 to 256, as said below
- anchors: int32 [3, 3072], P(None, ('wide', 'narrow')), may hold values from 0 to 1023, as said below
- helpers: int32 [3072, 1], P(('wide', 'narrow')), may hold values from 0 to 15, as said below
Outputs:
- spectrum: float32 [2, 128, 1024, 1024], P(None, 'wide', 'narrow')
- helper_load: float32 [16, 16], P('wide', 'narrow')
Inputs may be any that keep to these rules, and one draw needn't show every extreme that they name: `counts`: within each device's 12 bins the bins with a nonzero count come first; some device has all its bins nonzero. `helpers`: within each device's 12 bins at most 1 bins name the same helper. anchors[0] < 8, anchors[1] < 64, anchors[2] < 1024.
All inputs are finite; a program needn't handle non-finite values.
Results may differ from a plain program's by a relative error of at most 0.0054.
Values may be sent and summed in bfloat16 or wider, within the bound.
No kernel may reach another device: no remote copies, remote signals or barrier semaphores. Data moves between devices by JAX's collectives and lax.ppermute only.
A program may use at most 128 MiB of HBM per device.

v0:
```python
import math

import jax
import jax.numpy as jnp
from jax import lax
from jax.sharding import PartitionSpec as P

XS = 8
NY = 1024
NZ = 1024
PATCH = 24


spread_rate = 0.08
two_pi = 2.0 * math.pi
highest = lax.Precision.HIGHEST


def shifted(block, axis, distance):
    devices = range(lax.axis_size(axis))
    route = [((i - distance) % len(devices), i) for i in devices]
    return lax.ppermute(block, axis, route)


def make_patches(places, strength):
    cell_index = jnp.arange(PATCH, dtype=jnp.float32)
    profile = jnp.exp(-spread_rate * (cell_index[None, None, None, :] - places[:, :, :, None]) ** 2)
    left_side = strength[:, :, None] * profile[:, 0]
    right_side = (profile[:, 1, :, :, None] * profile[:, 2, :, None, :]).reshape(
        strength.shape[0], strength.shape[1], PATCH * PATCH
    )
    patch = jnp.einsum("cbi,cbj->cij", left_side, right_side, precision=highest)
    return patch.reshape(strength.shape[0], PATCH**3)


def skip_patches(places, strength):
    return jnp.zeros((strength.shape[0], PATCH**3), jnp.float32)


def source_patches(source):
    places, strength, number = source
    return lax.cond(jnp.any(number > 0), make_patches, skip_patches, places, strength)


def spread_items(received):
    places, strength, number = received
    patches = lax.map(source_patches, (places, strength, number))
    returned = lax.all_to_all(
        patches.astype(jnp.bfloat16), "narrow", split_axis=0, concat_axis=0, tiled=True
    )
    return (returned, jnp.sum(number, axis=0, keepdims=True))


def dft_tables(length, columns):
    ordinal = jnp.arange(length, dtype=jnp.int32)
    phase = ordinal[:, None] * columns[None, :] % length
    angle = phase.astype(jnp.float32) * (two_pi / length)
    norm_scale = 1.0 / math.sqrt(length)
    return (
        (jnp.cos(angle) * norm_scale).astype(jnp.bfloat16),
        (jnp.sin(angle) * norm_scale).astype(jnp.bfloat16),
    )


def fold_rows(volume):
    own_rows = volume.shape[1] - PATCH
    arrived = shifted(volume[:, own_rows:].astype(jnp.bfloat16), "narrow", 1).astype(jnp.float32)
    return volume[:, :own_rows].at[:, :PATCH].add(arrived)


def fold_planes(volume):
    ghost_slabs = volume.shape[0] // XS - 1
    pieces = volume.reshape(ghost_slabs + 1, XS, volume.shape[1], volume.shape[2])
    summed = pieces[0]
    for offset in range(1, ghost_slabs + 1):
        summed = summed + shifted(pieces[offset], "wide", offset)
    return summed


def along_y(values, table):
    return jnp.einsum("cyk,yv->ckv", values, table, preferred_element_type=jnp.float32)


def body(positions, forces, counts, anchors, helpers):
    bin_count = positions.shape[0]
    particles = positions.shape[2]
    helper_count = lax.axis_size("narrow")
    capacity = -(-bin_count // helper_count)
    slot_count = helper_count * capacity
    own_rows = NY // helper_count
    ghost_slabs = (PATCH + XS - 2) // XS
    route_list = helpers[:, 0]
    onehot = (route_list[:, None] == jnp.arange(helper_count, dtype=jnp.int32)[None, :]).astype(
        jnp.int32
    )
    before = jnp.cumsum(onehot, axis=0) - onehot
    ranking = jnp.sum(before * onehot, axis=1)
    target = route_list * capacity + ranking
    select = (target[None, :] == jnp.arange(slot_count, dtype=jnp.int32)[:, None]).astype(
        jnp.float32
    )
    live_mask = jnp.arange(particles, dtype=jnp.int32)[None, :] < counts[:, None]
    masked = jnp.where(live_mask, forces, jnp.zeros_like(forces))
    send_pos = jnp.dot(select, positions.reshape(bin_count, 3 * particles), precision=highest)
    send_pos = send_pos.reshape(helper_count, capacity, 3, particles)
    send_frc = jnp.dot(select, masked, precision=highest).reshape(helper_count, capacity, particles)
    send_cnt = jnp.dot(select, counts.astype(jnp.float32), precision=highest).reshape(
        helper_count, capacity
    )
    returned, work_load = spread_items(
        (
            lax.all_to_all(send_pos, "narrow", split_axis=0, concat_axis=0, tiled=True),
            lax.all_to_all(send_frc, "narrow", split_axis=0, concat_axis=0, tiled=True),
            lax.all_to_all(send_cnt, "narrow", split_axis=0, concat_axis=0, tiled=True),
        )
    )
    helper_load = (jnp.sum(work_load) / particles).reshape(1, 1)
    own_patches = jnp.dot(
        select.T.astype(jnp.bfloat16),
        returned.reshape(slot_count, PATCH**3),
        preferred_element_type=jnp.float32,
    )
    extent = jnp.zeros((XS * (ghost_slabs + 1), own_rows + PATCH, NZ + PATCH), jnp.float32)

    def place(bin_index, extent):
        corner = (anchors[0, bin_index], anchors[1, bin_index], anchors[2, bin_index])
        region = lax.dynamic_slice(extent, corner, (PATCH, PATCH, PATCH))
        return lax.dynamic_update_slice(
            extent, region + own_patches[bin_index].reshape(PATCH, PATCH, PATCH), corner
        )

    extent = lax.fori_loop(0, bin_count, place, extent)
    wrapped = extent[:, :, :NZ].at[:, :, :PATCH].add(extent[:, :, NZ:])
    grid_sum = fold_planes(fold_rows(wrapped))
    block_rows = NZ // helper_count
    slot_index = jnp.arange(NZ, dtype=jnp.int32)
    column_order = slot_index % block_rows * helper_count + slot_index // block_rows
    cos_z, sin_z = dft_tables(NZ, column_order)
    flat_rows = grid_sum.reshape(XS * own_rows, NZ).astype(jnp.bfloat16)
    z_real = (
        jnp.dot(flat_rows, cos_z, preferred_element_type=jnp.float32)
        .astype(jnp.bfloat16)
        .reshape(XS, own_rows, NZ)
    )
    z_imag = (
        (-jnp.dot(flat_rows, sin_z, preferred_element_type=jnp.float32))
        .astype(jnp.bfloat16)
        .reshape(XS, own_rows, NZ)
    )
    cos_y, sin_y = dft_tables(NY, jnp.arange(NY, dtype=jnp.int32))
    real_part = lax.all_to_all(z_real, "narrow", split_axis=2, concat_axis=1, tiled=True)
    imag_part = lax.all_to_all(z_imag, "narrow", split_axis=2, concat_axis=1, tiled=True)
    out_real = along_y(real_part, cos_y) + along_y(imag_part, sin_y)
    out_imag = along_y(imag_part, cos_y) - along_y(real_part, sin_y)
    spectrum = jnp.stack([out_real, out_imag])
    return (spectrum, helper_load)


def solution(mesh):
    return jax.shard_map(
        body,
        mesh=mesh,
        in_specs=(
            P(("wide", "narrow"), None, None),
            P(("wide", "narrow"), None),
            P(("wide", "narrow")),
            P(None, ("wide", "narrow")),
            P(("wide", "narrow"), None),
        ),
        out_specs=(P(None, "wide", "narrow", None), P("wide", "narrow")),
        check_vma=False,
    )
```

profile of v0, /device:TPU:1, one launch (start us, length us, event | category | flops | bytes accessed | tf_op | source)
XLA Modules:
  0.0 689.4 jit_solution(3785978357936552414)
XLA Ops:
  43.7 25.5 %while.25 = (s32[]{:T(128)}, bf16[16,1,13824]{2,1,0:T(2,128)(2,1)S(1)}, f32[16,1]{0,1:T(1,128)S(1)}, f32[16,1,256]{2,1,0:T(1,128)S(1)}, f32[16,1,3,256]{3,2,1,0:T(4,128)S(1)}, /*index=5*/s32[]{:T(128)}) while((s32[]{:T(128)}, bf16[16,1,13824]{2,1,0:T(2,128)(2,1)S(1)}, f32[16,1]{0,1:T(1,128)S(1)}, f32[16,1,256]{2,1,0:T(1,128)S(1)}, ...), condition=%wide.region_5.6_spmd, body=%wide.region_2.5_spmd.sunk | while | flops 42676228 | bytes 1631359 | solution.py:47
  78.5 15.5 %all-to-all-done.3 = bf16[16,2,6912]{2,1,0:T(2,128)(2,1)S(1)} async-done(((bf16[16,2,6912]{2,1,0:T(2,128)(2,1)}), bf16[16,2,6912]{2,1,0:T(2,128)(2,1)S(1)}, u32[]{:S(2)}, u32[]{:S(2)}) %all-to-all-start.3) | async-done | bytes 442400 | tf_op jit(solution)/shard_map/all_to_all | solution.py:48
  100.2 253.6 %while.26 = (s32[]{:T(128)}, f32[32,88,1048]{2,1,0:T(8,128)}, s32[3,12]{1,0:T(4,128)S(1)}, f32[12,13824]{1,0:T(8,128)S(1)}, s32[]{:T(128)}, /*index=5*/s32[]{:T(128)}, s32[]{:T(128)}, s32[]{:T(128)}, s32[]{:T(128)}) while((s32[]{:T(128)}, f32[32,88,1048]{2,1,0:T(8,128)}, s32[3,12]{1,0:T(4,128)S(1)}, f32[12,13824]{1,0:T(8,128)S(1)}, s32[]{:T(128)}, ...), condition=%wide.region_7.8_spmd, body=%wide.region_6.7_spmd.sunk | while | flops 13835 | bytes 497907 | solution.py:132
  108.2 13.2 %dynamic_update_slice.15 = f32[32,88,1048]{2,1,0:T(8,128)} dynamic-update-slice(f32[32,88,1048]{2,1,0:T(8,128)} %get-tuple-element.308, f32[24,24,24]{2,1,0:T(8,128)S(1)} %dynamic-slice_add_fusion.2, s32[]{:T(128)S(6)} %select_n.128, s32[]{:T(128)S(6)} %select_n.129, s32[]{:T(128)S(6)} %select_n.130) | dynamic-update-slice | bytes 110596 | tf_op jit(solution)/shard_map/while/body/eval_jaxpr/dynamic_update_slice | solution.py:128
  129.4 13.2 %dynamic_update_slice.15 = f32[32,88,1048]{2,1,0:T(8,128)} dynamic-update-slice(f32[32,88,1048]{2,1,0:T(8,128)} %get-tuple-element.308, f32[24,24,24]{2,1,0:T(8,128)S(1)} %dynamic-slice_add_fusion.2, s32[]{:T(128)S(6)} %select_n.128, s32[]{:T(128)S(6)} %select_n.129, s32[]{:T(128)S(6)} %select_n.130) | dynamic-update-slice | bytes 110596 | tf_op jit(solution)/shard_map/while/body/eval_jaxpr/dynamic_update_slice | solution.py:128
  150.6 13.2 %dynamic_update_slice.15 = f32[32,88,1048]{2,1,0:T(8,128)} dynamic-update-slice(f32[32,88,1048]{2,1,0:T(8,128)} %get-tuple-element.308, f32[24,24,24]{2,1,0:T(8,128)S(1)} %dynamic-slice_add_fusion.2, s32[]{:T(128)S(6)} %select_n.128, s32[]{:T(128)S(6)} %select_n.129, s32[]{:T(128)S(6)} %select_n.130) | dynamic-update-slice | bytes 110596 | tf_op jit(solution)/shard_map/while/body/eval_jaxpr/dynamic_update_slice | solution.py:128
  171.8 13.2 %dynamic_update_slice.15 = f32[32,88,1048]{2,1,0:T(8,128)} dynamic-update-slice(f32[32,88,1048]{2,1,0:T(8,128)} %get-tuple-element.308, f32[24,24,24]{2,1,0:T(8,128)S(1)} %dynamic-slice_add_fusion.2, s32[]{:T(128)S(6)} %select_n.128, s32[]{:T(128)S(6)} %select_n.129, s32[]{:T(128)S(6)} %select_n.130) | dynamic-update-slice | bytes 110596 | tf_op jit(solution)/shard_map/while/body/eval_jaxpr/dynamic_update_slice | solution.py:128
  192.9 13.1 %dynamic_update_slice.15 = f32[32,88,1048]{2,1,0:T(8,128)} dynamic-update-slice(f32[32,88,1048]{2,1,0:T(8,128)} %get-tuple-element.308, f32[24,24,24]{2,1,0:T(8,128)S(1)} %dynamic-slice_add_fusion.2, s32[]{:T(128)S(6)} %select_n.128, s32[]{:T(128)S(6)} %select_n.129, s32[]{:T(128)S(6)} %select_n.130) | dynamic-update-slice | bytes 110596 | tf_op jit(solution)/shard_map/while/body/eval_jaxpr/dynamic_update_slice | solution.py:128
  214.0 13.2 %dynamic_update_slice.15 = f32[32,88,1048]{2,1,0:T(8,128)} dynamic-update-slice(f32[32,88,1048]{2,1,0:T(8,128)} %get-tuple-element.308, f32[24,24,24]{2,1,0:T(8,128)S(1)} %dynamic-slice_add_fusion.2, s32[]{:T(128)S(6)} %select_n.128, s32[]{:T(128)S(6)} %select_n.129, s32[]{:T(128)S(6)} %select_n.130) | dynamic-update-slice | bytes 110596 | tf_op jit(solution)/shard_map/while/body/eval_jaxpr/dynamic_update_slice | solution.py:128
  256.1 13.0 %dynamic_update_slice.15 = f32[32,88,1048]{2,1,0:T(8,128)} dynamic-update-slice(f32[32,88,1048]{2,1,0:T(8,128)} %get-tuple-element.308, f32[24,24,24]{2,1,0:T(8,128)S(1)} %dynamic-slice_add_fusion.2, s32[]{:T(128)S(6)} %select_n.128, s32[]{:T(128)S(6)} %select_n.129, s32[]{:T(128)S(6)} %select_n.130) | dynamic-update-slice | bytes 110596 | tf_op jit(solution)/shard_map/while/body/eval_jaxpr/dynamic_update_slice | solution.py:128
  277.0 13.2 %dynamic_update_slice.15 = f32[32,88,1048]{2,1,0:T(8,128)} dynamic-update-slice(f32[32,88,1048]{2,1,0:T(8,128)} %get-tuple-element.308, f32[24,24,24]{2,1,0:T(8,128)S(1)} %dynamic-slice_add_fusion.2, s32[]{:T(128)S(6)} %select_n.128, s32[]{:T(128)S(6)} %select_n.129, s32[]{:T(128)S(6)} %select_n.130) | dynamic-update-slice | bytes 110596 | tf_op jit(solution)/shard_map/while/body/eval_jaxpr/dynamic_update_slice | solution.py:128
  298.2 13.2 %dynamic_update_slice.15 = f32[32,88,1048]{2,1,0:T(8,128)} dynamic-update-slice(f32[32,88,1048]{2,1,0:T(8,128)} %get-tuple-element.308, f32[24,24,24]{2,1,0:T(8,128)S(1)} %dynamic-slice_add_fusion.2, s32[]{:T(128)S(6)} %select_n.128, s32[]{:T(128)S(6)} %select_n.129, s32[]{:T(128)S(6)} %select_n.130) | dynamic-update-slice | bytes 110596 | tf_op jit(solution)/shard_map/while/body/eval_jaxpr/dynamic_update_slice | solution.py:128
  319.4 13.2 %dynamic_update_slice.15 = f32[32,88,1048]{2,1,0:T(8,128)} dynamic-update-slice(f32[32,88,1048]{2,1,0:T(8,128)} %get-tuple-element.308, f32[24,24,24]{2,1,0:T(8,128)S(1)} %dynamic-slice_add_fusion.2, s32[]{:T(128)S(6)} %select_n.128, s32[]{:T(128)S(6)} %select_n.129, s32[]{:T(128)S(6)} %select_n.130) | dynamic-update-slice | bytes 110596 | tf_op jit(solution)/shard_map/while/body/eval_jaxpr/dynamic_update_slice | solution.py:128
  340.6 13.2 %dynamic_update_slice.15 = f32[32,88,1048]{2,1,0:T(8,128)} dynamic-update-slice(f32[32,88,1048]{2,1,0:T(8,128)} %get-tuple-element.308, f32[24,24,24]{2,1,0:T(8,128)S(1)} %dynamic-slice_add_fusion.2, s32[]{:T(128)S(6)} %select_n.128, s32[]{:T(128)S(6)} %select_n.129, s32[]{:T(128)S(6)} %select_n.130) | dynamic-update-slice | bytes 110596 | tf_op jit(solution)/shard_map/while/body/eval_jaxpr/dynamic_update_slice | solution.py:128
  381.5 13.1 %collective-permute-done = bf16[32,24,1024]{2,1,0:T(8,128)(2,1)S(1)} collective-permute-done((bf16[32,24,1024]{2,1,0:T(8,128)(2,1)S(1)}, bf16[32,24,1024]{2,1,0:T(8,128)(2,1)S(1)}, u32[]{:S(2)}, u32[]{:S(2)}) %collective-permute-start) | collective-permute-done | bytes 1572896 | tf_op jit(solution)/shard_map/ppermute | solution.py:22
  404.2 41.8 %collective-permute-done.1 = f32[8,64,1024]{2,1,0:T(8,128)S(1)} collective-permute-done((f32[8,64,1024]{2,1,0:T(8,128)S(1)}, f32[8,64,1024]{2,1,0:T(8,128)S(1)}, u32[]{:S(2)}, u32[]{:S(2)}) %collective-permute-start.1) | collective-permute-done | bytes 2097184 | tf_op jit(solution)/shard_map/ppermute | solution.py:22
  445.9 67.2 %collective-permute-done.2 = f32[8,64,1024]{2,1,0:T(8,128)S(1)} collective-permute-done((f32[8,64,1024]{2,1,0:T(8,128)S(1)}, f32[8,64,1024]{2,1,0:T(8,128)S(1)}, u32[]{:S(2)}, u32[]{:S(2)}) %collective-permute-start.2) | collective-permute-done | bytes 2097184 | tf_op jit(solution)/shard_map/ppermute | solution.py:22
  513.1 22.0 %collective-permute-done.3 = f32[8,64,1024]{2,1,0:T(8,128)S(1)} collective-permute-done((f32[8,64,1024]{2,1,0:T(8,128)S(1)}, f32[8,64,1024]{2,1,0:T(8,128)S(1)}, u32[]{:S(2)}, u32[]{:S(2)}) %collective-permute-start.3) | collective-permute-done | bytes 2097184 | tf_op jit(solution)/shard_map/ppermute | solution.py:22
  536.2 16.7 %negate_convert_fusion = bf16[512,1024]{1,0:T(8,128)(2,1)S(1)} fusion(bf16[512,1024]{1,0:T(8,128)(2,1)S(1)} %bitcast.111, s32[1024]{0:T(1024)S(1)} %fusion.59), kind=kOutput, calls=%fused_computation.56 | convolution fusion | flops 1091567616 | bytes 2101248 | tf_op jit(solution)/shard_map/dot_general | solution.py:146
  565.5 18.5 %fusion.41 = bf16[512,1024]{1,0:T(8,128)(2,1)} fusion(bf16[512,1024]{1,0:T(8,128)(2,1)} %bitcast.112, s32[1024]{0:T(1024)S(1)} %fusion.59), kind=kOutput, calls=%fused_computation.63 | convolution fusion | flops 1091043328 | bytes 2101248 | tf_op jit(solution)/shard_map/dot_general | solution.py:141
  606.0 17.5 %fusion.29 = f32[8,64,1024]{2,1,0:T(8,128)} fusion(bf16[8,1024,64]{1,2,0:T(8,128)(2,1)S(1)} %all_to_all.56), kind=kOutput, calls=%fused_computation.60 | convolution fusion | flops 1090519040 | bytes 3145728 | tf_op jit(solution)/shard_map/cyk,yv->ckv/dot_general | solution.py:81
  635.0 16.9 %fusion.27 = f32[8,64,1024]{2,1,0:T(8,128)S(1)} fusion(bf16[8,1024,64]{1,2,0:T(8,128)(2,1)S(1)} %all_to_all.52), kind=kOutput, calls=%fused_computation.59 | convolution fusion | flops 1090519040 | bytes 3145728 | tf_op jit(solution)/shard_map/cyk,yv->ckv/dot_general | solution.py:81
  652.0 16.8 %add_bitcast_fusion = f32[1,8,64,1024]{3,2,1,0:T(8,128)S(1)} fusion(f32[8,64,1024]{2,1,0:T(8,128)S(1)} %copy-done.2, bf16[8,1024,64]{1,2,0:T(8,128)(2,1)S(1)} %all_to_all.52), kind=kOutput, calls=%fused_computation.55 | convolution fusion | flops 1091043328 | bytes 5242880 | tf_op jit(solution)/shard_map/cyk,yv->ckv/dot_general | solution.py:81
  668.8 17.0 %subtract_bitcast_fusion = f32[1,8,64,1024]{3,2,1,0:T(8,128)S(1)} fusion(f32[8,64,1024]{2,1,0:T(8,128)S(1)} %fusion.27, bf16[8,1024,64]{1,2,0:T(8,128)(2,1)S(1)} %all_to_all.56), kind=kOutput, calls=%fused_computation.54 | convolution fusion | flops 1091043328 | bytes 5242880 | tf_op jit(solution)/shard_map/cyk,yv->ckv/dot_general | solution.py:81
  (199 shorter events, 203.3 us)
Async XLA Ops:
  4.3 17.0 %all-to-all-start = ((f32[16,1,1]{2,1,0:T(1,128)}), f32[16,1,1]{2,1,0:T(1,128)S(1)}, u32[]{:S(2)}, u32[]{:S(2)}) async-start(f32[16,1,1]{2,1,0:T(1,128)} %bitcast.34), calls=%async_computation | async-start | bytes 16384 | tf_op jit(solution)/shard_map/all_to_all | solution.py:114
  21.3 11.4 %all-to-all-start.2 = ((f32[16,1,3,256]{3,1,2,0:T(1,128)}), f32[16,1,3,256]{3,1,2,0:T(1,128)S(1)}, u32[]{:S(2)}, u32[]{:S(2)}) async-start(f32[16,1,3,256]{3,1,2,0:T(1,128)} %copy.45), calls=%async_computation.2 | async-start | bytes 98304 | tf_op jit(solution)/shard_map/all_to_all | solution.py:112
  32.7 11.0 %all-to-all-start.1 = ((f32[16,1,256]{2,1,0:T(1,128)}), f32[16,1,256]{2,1,0:T(1,128)S(1)}, u32[]{:S(2)}, u32[]{:S(2)}) async-start(f32[16,1,256]{2,1,0:T(1,128)} %copy.43), calls=%async_computation.1 | async-start | bytes 32768 | tf_op jit(solution)/shard_map/all_to_all | solution.py:113
  73.9 20.2 %all-to-all-start.3 = ((bf16[16,2,6912]{2,1,0:T(2,128)(2,1)}), bf16[16,2,6912]{2,1,0:T(2,128)(2,1)S(1)}, u32[]{:S(2)}, u32[]{:S(2)}) async-start(bf16[16,2,6912]{2,1,0:T(2,128)(2,1)} %reshape.285), calls=%async_computation.3 | async-start | bytes 884736 | tf_op jit(solution)/shard_map/all_to_all | solution.py:48
  94.7 5.5 copy-start.1
  377.2 17.4 %collective-permute-start = (bf16[32,24,1024]{2,1,0:T(8,128)(2,1)S(1)}, bf16[32,24,1024]{2,1,0:T(8,128)(2,1)S(1)}, u32[]{:S(2)}, u32[]{:S(2)}) collective-permute-start(bf16[32,24,1024]{2,1,0:T(8,128)(2,1)S(1)} %slice.135), channel_id=1, source_target_pairs={{15,0},{0,1},{1,2},{2,3},{3,4},{4,5},{5,6},{6,7},{7,8},{8,9},{9,10... | collective-permute-start | bytes 4718600 | tf_op jit(solution)/shard_map/ppermute | solution.py:22
  397.8 48.1 %collective-permute-start.1 = (f32[8,64,1024]{2,1,0:T(8,128)S(1)}, f32[8,64,1024]{2,1,0:T(8,128)S(1)}, u32[]{:S(2)}, u32[]{:S(2)}) collective-permute-start(f32[8,64,1024]{2,1,0:T(8,128)S(1)} %get-tuple-element.215), channel_id=1, source_target_pairs={{240,0},{0,16},{16,32},{32,48},{48,64},{64,80},{80,96},{96,112},{1... | collective-permute-start | bytes 6291464 | tf_op jit(solution)/shard_map/ppermute | solution.py:22
  398.3 114.8 %collective-permute-start.2 = (f32[8,64,1024]{2,1,0:T(8,128)S(1)}, f32[8,64,1024]{2,1,0:T(8,128)S(1)}, u32[]{:S(2)}, u32[]{:S(2)}) collective-permute-start(f32[8,64,1024]{2,1,0:T(8,128)S(1)} %get-tuple-element.217), channel_id=1, source_target_pairs={{224,0},{240,16},{0,32},{16,48},{32,64},{48,80},{64,96},{80,112},{... | collective-permute-start | bytes 6291464 | tf_op jit(solution)/shard_map/ppermute | solution.py:22
  400.9 134.2 %collective-permute-start.3 = (f32[8,64,1024]{2,1,0:T(8,128)S(1)}, f32[8,64,1024]{2,1,0:T(8,128)S(1)}, u32[]{:S(2)}, u32[]{:S(2)}) collective-permute-start(f32[8,64,1024]{2,1,0:T(8,128)S(1)} %get-tuple-element.216), channel_id=1, source_target_pairs={{208,0},{224,16},{240,32},{0,48},{16,64},{32,80},{48,96},{64,112},... | collective-permute-start | bytes 6291464 | tf_op jit(solution)/shard_map/ppermute | solution.py:22
  536.1 16.7 %copy-start = (bf16[8,64,1024]{2,1,0:T(8,128)(2,1)}, bf16[8,64,1024]{2,1,0:T(8,128)(2,1)S(1)}, u32[]{:S(2)}) copy-start(bf16[8,64,1024]{2,1,0:T(8,128)(2,1)S(1)} %fusion.24) | copy-start | bytes 3145732
  556.8 36.6 %all-to-all-start.5 = ((bf16[16,2,16384]{2,1,0:T(2,128)(2,1)}), bf16[16,2,16384]{2,1,0:T(2,128)(2,1)S(1)}, u32[]{:S(2)}, u32[]{:S(2)}) async-start(bf16[16,2,16384]{2,1,0:T(2,128)(2,1)} %reshape.289), calls=%async_computation.5 | async-start | bytes 2097152 | tf_op jit(solution)/shard_map/all_to_all | solution.py:152
  593.4 32.0 %all-to-all-start.4 = ((bf16[16,2,16384]{2,1,0:T(2,128)(2,1)}), bf16[16,2,16384]{2,1,0:T(2,128)(2,1)}, u32[]{:S(2)}, u32[]{:S(2)}) async-start(bf16[16,2,16384]{2,1,0:T(2,128)(2,1)} %reshape.287), calls=%async_computation.4 | async-start | bytes 2097152 | tf_op jit(solution)/shard_map/all_to_all | solution.py:151
  635.0 17.0 %copy-start.2 = (f32[8,64,1024]{2,1,0:T(8,128)S(1)}, f32[8,64,1024]{2,1,0:T(8,128)}, u32[]{:S(2)}) copy-start(f32[8,64,1024]{2,1,0:T(8,128)} %fusion.29) | copy-start | bytes 6291460
where the time goes:
time: 699 us; the launch traced here: 689 us
  local copies, waits for them, and re-layouts  233 us (33%)
  waiting for transfers between devices  184 us (26%)
  matrix products  109 us (16%)
  loops' own time  79.4 us (11%)
  starting transfers between devices  41.8 us (6%)
  other arithmetic  39.3 us (6%)
    dynamic_update_slice x12, local copies, waits for them, and re-layouts, place(): lax.dynamic_update_slice(extent, region + own_patches[bin_index].reshape(...  158 us
    ppermute x4, waiting for transfers between devices, shifted(): return lax.ppermute(block, axis, route)  144 us
    another operation x1, loops' own time, body(): extent = lax.fori_loop(0, bin_count, place, extent)  68.2 us
    dot_general x4, matrix products, along_y(): jnp.einsum('cyk,yv->ckv', values, table, preferred_element_type=jnp.float32)  68.1 us
    dot_general x1, matrix products, body(): jnp.dot(flat_rows, cos_z, preferred_element_type=jnp.float32)  18.5 us
    dot_general x1, matrix products, body(): jnp.dot(flat_rows, sin_z, preferred_element_type=jnp.float32)  16.7 us
    add x12, other arithmetic, place(): region + own_patches[bin_index].reshape(PATCH, PATCH, PATCH)  15.7 us
    all_to_all x1, waiting for transfers between devices, spread_items(): lax.all_to_all(patches.astype(jnp.bfloat16), 'narrow', split_axis=0, conc...  15.5 us
  transfers between devices with their start and end apart: 10, of which 10 were waited for; matrix products, arithmetic and copies ran while one was open for 8% of the time, Pallas kernels for 0%

commit v1 on v0

v1 whole, which is shorter than its diff:
```python
import functools
import math

import jax
import jax.numpy as jnp
import ml_dtypes
import numpy as np
from jax import lax
from jax.experimental import pallas as pl
from jax.experimental.pallas import tpu as pltpu
from jax.sharding import PartitionSpec as P

XS = 8
NY = 1024
NZ = 1024
PATCH = 24
BIN = 256
BINS_DEV = 12
SLABS = 4
CHIPS = 8
SOURCES = SLABS * CHIPS
ROWS = 56
META = 4 * BINS_DEV
RATE = 0.08
LOW = 6.0
STEP = 12.0 / 65535.0
TOP = 32767.0
TILES = 4
LANES = 128
UNROLL = 2
ENTRIES = SOURCES * BINS_DEV + UNROLL


@functools.lru_cache(maxsize=None)
def tables():
    ordinal = np.arange(NZ)
    phase = ordinal[:, None] * ordinal[None, :] % NZ
    angle = phase.astype(np.float64) * (2.0 * math.pi / NZ)
    cos = (np.cos(angle) / math.sqrt(NZ)).astype(ml_dtypes.bfloat16)
    sin = (np.sin(angle) / math.sqrt(NZ)).astype(ml_dtypes.bfloat16)
    cz = cos.reshape(NZ, 64, 16).transpose(2, 0, 1)
    sz = sin.reshape(NZ, 64, 16).transpose(2, 0, 1)
    both = np.concatenate([cz, -sz], axis=2)
    z_table = both.reshape(CHIPS, 2, NZ, LANES).transpose(0, 2, 1, 3).reshape(CHIPS, NZ, 2 * LANES)
    width = NY // TILES
    y_table = np.stack(
        [
            np.concatenate([cos[:, t * width : (t + 1) * width], sin[:, t * width : (t + 1) * width]], axis=1)
            for t in range(TILES)
        ]
    )
    return np.ascontiguousarray(z_table), np.ascontiguousarray(y_table)


def pack_kernel(counts, anchors, helpers, home, positions, forces, out):
    bins = lax.broadcasted_iota(jnp.int32, (BINS_DEV, BIN), 0)
    slot = lax.broadcasted_iota(jnp.int32, (BINS_DEV, BIN), 1)
    limit = jnp.zeros((BINS_DEV, BIN), jnp.int32)
    for b in range(BINS_DEV):
        limit = jnp.where(bins == b, counts[b], limit)
    live = jnp.where(slot < limit, forces[...], 0.0)
    largest = jnp.max(jnp.abs(live), axis=1, keepdims=True)
    power = jnp.clip(jnp.ceil(jnp.log(largest) * (1.0 / math.log(2.0))), -126.0, 1.0)
    scaled = live * jnp.exp2(-power) * TOP
    code = jnp.clip(jnp.floor(scaled + 0.5), -TOP, TOP).astype(jnp.int32)
    exponent = power.astype(jnp.int32)
    lane = lax.broadcasted_iota(jnp.int32, (1, LANES), 1)
    meta = jnp.zeros((1, LANES), jnp.int32)
    for b in range(BINS_DEV):
        place = jnp.clip((positions[b] - LOW) * (1.0 / STEP) + 0.5, 0.0, 65535.0).astype(jnp.int32)
        first = place[0:1] | (place[1:2] << 16)
        second = place[2:3] | (code[b : b + 1] << 16)
        out[4 * b : 4 * b + 1, :] = first[:, :LANES]
        out[4 * b + 1 : 4 * b + 2, :] = first[:, LANES:]
        out[4 * b + 2 : 4 * b + 3, :] = second[:, :LANES]
        out[4 * b + 3 : 4 * b + 4, :] = second[:, LANES:]
        meta = jnp.where(lane == b, counts[b], meta)
        meta = jnp.where(lane == 16 + b, home[0] * (NY // 16) + anchors[1, b], meta)
        meta = jnp.where(lane == 32 + b, anchors[0, b], meta)
        meta = jnp.where(lane == 48 + b, anchors[2, b], meta)
        meta = jnp.where(lane == 64 + b, helpers[b, 0], meta)
        meta = jnp.where(lane == 80 + b, exponent[b : b + 1, 0:1], meta)
    out[META:ROWS, :] = jnp.broadcast_to(meta, (ROWS - META, LANES))


def pack(positions, forces, counts, anchors, helpers, home):
    smem = pl.BlockSpec(memory_space=pltpu.SMEM)
    vmem = pl.BlockSpec(memory_space=pltpu.VMEM)
    return pl.pallas_call(
        pack_kernel,
        out_shape=jax.ShapeDtypeStruct((ROWS, LANES), jnp.int32),
        in_specs=[smem, smem, smem, smem, vmem, vmem],
        out_specs=vmem,
        name="pack",
    )(counts, anchors, helpers, home, positions, forces)


def spread_kernel(
    core, meta, scale, g0, g1, g2, g3, table, own, other,
    data, grid, wave, rows, offsets, ys, zs, scales,
):
    chunk = 64

    def clear(i, carry):
        at = pl.ds(pl.multiple_of(i * chunk, chunk), chunk)
        zero = jnp.zeros((chunk, LANES), jnp.float32)
        grid[0, at, :] = zero
        grid[1, at, :] = zero
        return carry

    lax.fori_loop(0, XS * (NY + PATCH) // chunk, clear, 0)
    for s, block in enumerate((g0, g1, g2, g3)):
        data[s * CHIPS * ROWS : (s + 1) * CHIPS * ROWS, :] = block[...]
    for c in range(2):
        lanes = slice(c * LANES, (c + 1) * LANES)
        wave[c, :NZ, :] = table[:, lanes].astype(jnp.float32)
        wave[c, NZ:, :] = table[:PATCH, lanes].astype(jnp.float32)

    def source(src, total):
        slab = src // CHIPS

        def more(state):
            b, _ = state
            return jnp.logical_and(b < BINS_DEV, meta[src, jnp.minimum(b, BINS_DEV - 1)] > 0)

        def add(state):
            b, k = state
            rows[k] = src * ROWS + 4 * b
            offsets[k] = XS * slab - meta[src, 32 + b]
            ys[k] = meta[src, 16 + b]
            zs[k] = meta[src, 48 + b]
            scales[k] = scale[src, b]
            return b + 1, k + 1

        return lax.while_loop(more, add, (jnp.int32(0), total))[1]

    total = lax.fori_loop(0, SOURCES, source, jnp.int32(0))
    for extra in range(UNROLL):
        rows[total + extra] = 0
        offsets[total + extra] = 0
        ys[total + extra] = 0
        zs[total + extra] = 0
        scales[total + extra] = jnp.float32(0.0)

    plane = lax.broadcasted_iota(jnp.int32, (XS, LANES), 0)
    cell = lax.broadcasted_iota(jnp.int32, (PATCH, LANES), 0).astype(jnp.float32)

    def one(k):
        row = rows[k]
        index = plane + offsets[k]
        inside = jnp.logical_and(index >= 0, index < PATCH)
        along_x = index.astype(jnp.float32)
        left, right = [], []
        for half in range(2):
            first = data[pl.ds(row + half, 1), :]
            second = data[pl.ds(row + 2 + half, 1), :]
            px = (first & 0xFFFF).astype(jnp.float32) * STEP + LOW
            py = ((first >> 16) & 0xFFFF).astype(jnp.float32) * STEP + LOW
            pz = (second & 0xFFFF).astype(jnp.float32) * STEP + LOW
            force = (second >> 16).astype(jnp.float32) * scales[k]
            ax = jnp.where(inside, jnp.exp(-RATE * (along_x - px) ** 2) * force, 0.0)
            ay = jnp.exp(-RATE * (cell - py) ** 2)
            az = jnp.exp(-RATE * (cell - pz) ** 2)
            left.append((ay[:, None, :] * ax[None, :, :]).reshape(PATCH * XS, LANES).astype(jnp.bfloat16))
            right.append(az.astype(jnp.bfloat16))
        patch = lax.dot_general(
            jnp.concatenate(left, axis=1),
            jnp.concatenate(right, axis=1),
            (((1,), (1,)), ((), ())),
            preferred_element_type=jnp.float32,
        ).astype(jnp.bfloat16)
        turn = jnp.concatenate([wave[c, pl.ds(zs[k], PATCH), :] for c in range(2)], axis=1)
        return jnp.dot(patch, turn.astype(jnp.bfloat16), preferred_element_type=jnp.float32)

    def several(i, carry):
        found = [one(UNROLL * i + u) for u in range(UNROLL)]
        for u in range(UNROLL):
            at = pl.ds(pl.multiple_of(ys[UNROLL * i + u] * XS, XS), PATCH * XS)
            grid[0, at, :] += found[u][:, :LANES]
            grid[1, at, :] += found[u][:, LANES:]
        return carry

    lax.fori_loop(0, (total + UNROLL - 1) // UNROLL, several, 0)
    grid[0, : PATCH * XS, :] += grid[0, NY * XS :, :]
    grid[1, : PATCH * XS, :] += grid[1, NY * XS :, :]
    mine = core[1]

    def finish(i, carry):
        for x in range(XS):
            at = pl.ds(i * chunk * XS + x, chunk, stride=XS)
            to = pl.ds(pl.multiple_of(i * chunk, chunk), chunk)
            own[x, to, :] = grid[mine, at, :].astype(jnp.bfloat16)
            other[x, to, :] = grid[1 - mine, at, :].astype(jnp.bfloat16)
        return carry

    lax.fori_loop(0, NY // chunk, finish, 0)


def spread(core, meta, scale, blocks, z_table):
    smem = pl.BlockSpec(memory_space=pltpu.SMEM)
    vmem = pl.BlockSpec(memory_space=pltpu.VMEM)
    half = jax.ShapeDtypeStruct((XS, NY, LANES), jnp.bfloat16)
    return pl.pallas_call(
        spread_kernel,
        out_shape=(half, half),
        grid_spec=pltpu.PrefetchScalarGridSpec(
            num_scalar_prefetch=3,
            grid=(1,),
            in_specs=[vmem] * 4 + [pl.BlockSpec((None, NZ, 2 * LANES), lambda i, core, meta, scale: (core[0], 0, 0))],
            out_specs=[vmem, vmem],
            scratch_shapes=[
                pltpu.VMEM((SOURCES * ROWS, LANES), jnp.int32),
                pltpu.VMEM((2, XS * (NY + PATCH), LANES), jnp.float32),
                pltpu.VMEM((2, NZ + PATCH, LANES), jnp.float32),
                pltpu.SMEM((ENTRIES,), jnp.int32),
                pltpu.SMEM((ENTRIES,), jnp.int32),
                pltpu.SMEM((ENTRIES,), jnp.int32),
                pltpu.SMEM((ENTRIES,), jnp.int32),
                pltpu.SMEM((ENTRIES,), jnp.float32),
            ],
        ),
        compiler_params=pltpu.CompilerParams(vmem_limit_bytes=48 * 2**20),
        name="spread",
    )(core, meta, scale, *blocks, z_table)


def rows_kernel(own, other, table, out, lines):
    @pl.when(pl.program_id(0) == 0)
    def _():
        for x in range(XS):
            both = own[x].astype(jnp.float32) + other[x].astype(jnp.float32)
            lines[x * LANES : (x + 1) * LANES, :] = both.astype(jnp.bfloat16).T

    width = NY // TILES
    waves = jnp.dot(lines[...], table[...], preferred_element_type=jnp.float32)
    for x in range(XS):
        real = waves[x * LANES : x * LANES + 64]
        imag = waves[x * LANES + 64 : (x + 1) * LANES]
        out[0, x] = real[:, :width] + imag[:, width:]
        out[1, x] = imag[:, :width] - real[:, width:]


def along_rows(own, other, y_table):
    width = NY // TILES
    vmem = pl.BlockSpec(memory_space=pltpu.VMEM)
    return pl.pallas_call(
        rows_kernel,
        out_shape=jax.ShapeDtypeStruct((2, XS, 64, NY), jnp.float32),
        grid=(TILES,),
        in_specs=[vmem, vmem, pl.BlockSpec((None, NY, 2 * width), lambda t: (t, 0, 0))],
        out_specs=pl.BlockSpec((2, XS, 64, width), lambda t: (0, 0, 0, t)),
        scratch_shapes=[pltpu.VMEM((XS * LANES, NY), jnp.bfloat16)],
        compiler_params=pltpu.CompilerParams(vmem_limit_bytes=48 * 2**20),
        name="rows",
    )(own, other, y_table)


def slab_shift(block, distance):
    count = lax.axis_size("wide")
    return lax.ppermute(block, "wide", [(i, (i + distance) % count) for i in range(count)])


def chip_shift(block, distance):
    count = lax.axis_size("narrow")
    return lax.ppermute(block, "narrow", [(i, (i + 2 * distance) % count) for i in range(count)])


def partner(block):
    count = lax.axis_size("narrow")
    return lax.ppermute(block, "narrow", [(i, i ^ 1) for i in range(count)])


def ring(block):
    near = jnp.concatenate([chip_shift(block, 1), block, chip_shift(block, -1)], axis=0)
    before = chip_shift(near, 3)
    after = chip_shift(near[: 2 * ROWS], -3)
    return jnp.concatenate([near, before, after], axis=0)


def body(positions, forces, counts, anchors, helpers):
    z_table, y_table = tables()
    home = lax.axis_index("narrow").astype(jnp.int32)
    packed = pack(positions, forces, counts, anchors, helpers, home.reshape(1))
    block = ring(packed)
    blocks = [block] + [slab_shift(block, d) for d in range(1, SLABS)]
    meta = jnp.concatenate([g.reshape(CHIPS, ROWS, LANES)[:, META] for g in blocks], axis=0)
    scale = jnp.exp2(meta[:, 80:96].astype(jnp.float32)) * (1.0 / TOP)
    numbers, choice = meta[:CHIPS, :BINS_DEV], meta[:CHIPS, 64 : 64 + BINS_DEV]
    helper_index = jnp.arange(16, dtype=jnp.int32)
    matches = choice[:, :, None] == helper_index[None, None, :]
    load = jnp.sum(jnp.where(matches, numbers[:, :, None], 0), axis=(0, 1)).astype(jnp.float32)
    load = load + partner(load)
    helper_load = (jnp.sum(jnp.where(helper_index == home, load, 0.0)) / BIN).reshape(1, 1)
    core = jnp.stack([home // 2, home % 2])
    own, other = spread(core, meta, scale, blocks, jnp.asarray(z_table))
    spectrum = along_rows(own, partner(other), jnp.asarray(y_table))
    return (spectrum, helper_load)


def solution(mesh):
    return jax.shard_map(
        body,
        mesh=mesh,
        in_specs=(
            P(("wide", "narrow"), None, None),
            P(("wide", "narrow"), None),
            P(("wide", "narrow")),
            P(None, ("wide", "narrow")),
            P(("wide", "narrow"), None),
        ),
        out_specs=(P(None, "wide", "narrow", None), P("wide", "narrow")),
        check_vma=False,
    )
```

time: 699 us -> 105 us (0.15)
  the two profiles are of different devices: /device:TPU:1 before, /device:TPU:9 now
where the time goes in v1:
time: 105 us; the launch traced here: 106 us
  Pallas kernels  59 us (56%)
  waiting for transfers between devices  25.2 us (24%)
  starting transfers between devices  14.4 us (14%)
  other arithmetic  2.38 us (2%)
  between operations  2.38 us (2%)
  local copies, waits for them, and re-layouts  2.36 us (2%)
    pallas_call x1, Pallas kernels, spread(): pl.pallas_call(spread_kernel, out_shape=(half, half), grid_spec=pltpu.Pre...  48.4 us
    ppermute x3, waiting for transfers between devices, slab_shift(): lax.ppermute(block, 'wide', [(i, (i + distance) % count) for i in range(c...  13.9 us
    ppermute x4, starting transfers between devices, chip_shift(): lax.ppermute(block, 'narrow', [(i, (i + 2 * distance) % count) for i in r...  9.11 us
    pallas_call x1, Pallas kernels, along_rows(): pl.pallas_call(rows_kernel, out_shape=jax.ShapeDtypeStruct((2, XS, 64, NY...  8.96 us
    ppermute x4, waiting for transfers between devices, chip_shift(): lax.ppermute(block, 'narrow', [(i, (i + 2 * distance) % count) for i in r...  8.16 us
    ppermute x3, starting transfers between devices, slab_shift(): lax.ppermute(block, 'wide', [(i, (i + distance) % count) for i in range(c...  4.69 us
    ppermute x2, waiting for transfers between devices, partner(): return lax.ppermute(block, 'narrow', [(i, i ^ 1) for i in range(count)])  3.17 us
  transfers between devices with their start and end apart: 9, of which 6 were waited for; matrix products, arithmetic and copies ran while one was open for 3% of the time, Pallas kernels for 0%

profile of v1, /device:TPU:9, one launch (start us, length us, event | category | flops | bytes accessed | tf_op | source)
XLA Modules:
  0.0 105.7 jit_solution(8870128702315344367)
XLA Ops:
  0.6 1.3 %copy.14.helpers = s32[12,1]{1,0:T(8,128)} copy(s32[12,1]{0,1:T(1,128)} %param.11) | data formatting | bytes 96 | tf_op args[4]
  2.0 1.6 %pack.1 = s32[56,128]{1,0:T(8,128)} custom-call(s32[12]{0:T(128)} %counts.1, s32[3,12]{1,0:T(4,128)} %anchors.1, s32[12,1]{1,0:T(8,128)} %copy.14.helpers, s32[1]{0:T(128)} %bitcast.2.home, f32[12,3,256]{2,1,0:T(4,128)} %positions.1, f32[12,256]{1,0:T(8,128)} %forces.1), custom_call_target="tpu_custom_call" | custom-call | tf_op jit(solution)/shard_map/pack/pallas_call | solution.py:89
  3.6 1.6 %collective-permute-start = (s32[56,128]{1,0:T(8,128)}, s32[56,128]{1,0:T(8,128)S(1)}, u32[]{:S(2)}, u32[]{:S(2)}) collective-permute-start(s32[56,128]{1,0:T(8,128)} %pack.1), channel_id=1, source_target_pairs={{0,2},{1,3},{2,4},{3,5},{4,6},{5,7},{6,8},{7,9},{8,10},{9,11},{10,... | collective-permute-start | bytes 86024 | tf_op jit(solution)/shard_map/ppermute | solution.py:265
  5.2 3.9 %collective-permute-start.1 = (s32[56,128]{1,0:T(8,128)}, s32[56,128]{1,0:T(8,128)S(1)}, u32[]{:S(2)}, u32[]{:S(2)}) collective-permute-start(s32[56,128]{1,0:T(8,128)} %pack.1), channel_id=1, source_target_pairs={{0,14},{1,15},{2,0},{3,1},{4,2},{5,3},{6,4},{7,5},{8,6},{9,7},{10,... | collective-permute-start | bytes 86024 | tf_op jit(solution)/shard_map/ppermute | solution.py:265
  9.1 1.5 %collective-permute-done = s32[56,128]{1,0:T(8,128)S(1)} collective-permute-done((s32[56,128]{1,0:T(8,128)}, s32[56,128]{1,0:T(8,128)S(1)}, u32[]{:S(2)}, u32[]{:S(2)}) %collective-permute-start) | collective-permute-done | bytes 28704 | tf_op jit(solution)/shard_map/ppermute | solution.py:265
  10.6 0.8 pad_add_fusion.1
  11.4 2.4 %collective-permute-start.3 = (s32[112,128]{1,0:T(8,128)S(1)}, s32[112,128]{1,0:T(8,128)S(1)}, u32[]{:S(2)}, u32[]{:S(2)}) collective-permute-start(s32[112,128]{1,0:T(8,128)S(1)} %pad_add_fusion.1), channel_id=1, source_target_pairs={{0,10},{1,11},{2,12},{3,13},{4,14},{5,15},{6,0},{7,1},{8,2},{9,3},... | collective-permute-start | bytes 172040 | tf_op jit(solution)/shard_map/ppermute | solution.py:265
  13.7 0.8 pad_add_fusion
  14.5 1.2 %collective-permute-start.2 = (s32[168,128]{1,0:T(8,128)S(1)}, s32[168,128]{1,0:T(8,128)S(1)}, u32[]{:S(2)}, u32[]{:S(2)}) collective-permute-start(s32[168,128]{1,0:T(8,128)S(1)} %pad_add_fusion), channel_id=1, source_target_pairs={{0,6},{1,7},{2,8},{3,9},{4,10},{5,11},{6,12},{7,13},{8,14},{9,15},... | collective-permute-start | bytes 258056 | tf_op jit(solution)/shard_map/ppermute | solution.py:265
  15.7 0.8 constant_dynamic-update-slice_fusion.3
  16.4 6.7 %collective-permute-done.2 = s32[168,128]{1,0:T(8,128)S(1)} collective-permute-done((s32[168,128]{1,0:T(8,128)S(1)}, s32[168,128]{1,0:T(8,128)S(1)}, u32[]{:S(2)}, u32[]{:S(2)}) %collective-permute-start.2) | collective-permute-done | bytes 86048 | tf_op jit(solution)/shard_map/ppermute | solution.py:265
  23.1 2.6 %collective-permute-start.6 = (s32[448,128]{1,0:T(8,128)S(1)}, s32[448,128]{1,0:T(8,128)S(1)}, u32[]{:S(2)}, u32[]{:S(2)}) collective-permute-start(s32[448,128]{1,0:T(8,128)S(1)} %constant_dynamic-update-slice_fusion.g0), channel_id=1, source_target_pairs={{0,48},{16,64},{32,80},{48,96},{64,112},{80,128},{96,144},{112,160... | collective-permute-start | bytes 688136 | tf_op jit(solution)/shard_map/ppermute | solution.py:260
  25.7 1.5 %collective-permute-start.5 = (s32[448,128]{1,0:T(8,128)S(1)}, s32[448,128]{1,0:T(8,128)S(1)}, u32[]{:S(2)}, u32[]{:S(2)}) collective-permute-start(s32[448,128]{1,0:T(8,128)S(1)} %constant_dynamic-update-slice_fusion.g0), channel_id=1, source_target_pairs={{0,32},{16,48},{32,64},{48,80},{64,96},{80,112},{96,128},{112,144}... | collective-permute-start | bytes 688136 | tf_op jit(solution)/shard_map/ppermute | solution.py:260
  27.2 0.6 collective-permute-start.4
  27.9 1.1 %collective-permute-done.6.g3 = s32[448,128]{1,0:T(8,128)S(1)} collective-permute-done((s32[448,128]{1,0:T(8,128)S(1)}, s32[448,128]{1,0:T(8,128)S(1)}, u32[]{:S(2)}, u32[]{:S(2)}) %collective-permute-start.6) | collective-permute-done | bytes 229408 | tf_op jit(solution)/shard_map/ppermute | solution.py:260
  29.0 5.4 %collective-permute-done.5.g2 = s32[448,128]{1,0:T(8,128)S(1)} collective-permute-done((s32[448,128]{1,0:T(8,128)S(1)}, s32[448,128]{1,0:T(8,128)S(1)}, u32[]{:S(2)}, u32[]{:S(2)}) %collective-permute-start.5) | collective-permute-done | bytes 229408 | tf_op jit(solution)/shard_map/ppermute | solution.py:260
  34.4 7.5 %collective-permute-done.4.g1 = s32[448,128]{1,0:T(8,128)S(1)} collective-permute-done((s32[448,128]{1,0:T(8,128)S(1)}, s32[448,128]{1,0:T(8,128)S(1)}, u32[]{:S(2)}, u32[]{:S(2)}) %collective-permute-start.4) | collective-permute-done | bytes 229408 | tf_op jit(solution)/shard_map/ppermute | solution.py:260
  41.9 48.4 %spread.1 = (bf16[8,1024,128]{2,1,0:T(8,128)(2,1)S(1)}, bf16[8,1024,128]{2,1,0:T(8,128)(2,1)}) custom-call(s32[2]{0:T(128)S(1)} %pad_add_fusion.3.core, s32[32,128]{1,0:T(8,128)S(1)} %pad_add_fusion.2.meta, f32[32,16]{1,0:T(8,128)S(1)} %fusion.2.scale, s32[448,128]{1,0:T(8,128)S(1)} %constant_dynamic-update-slice_fusion.g0, ...), custom_call_target="tpu_custom_call" | custom-call | tf_op jit(solution)/shard_map/spread/pallas_call | solution.py:203
  90.4 0.1 copy.19
  90.6 0.1 select_reduce_fusion
  90.7 0.6 collective-permute-start.8
  91.3 3.2 %collective-permute-done.8 = f32[16]{0:T(128)S(1)} collective-permute-done((f32[16]{0:T(128)S(1)}, f32[16]{0:T(128)S(1)}, u32[]{:S(2)}, u32[]{:S(2)}) %collective-permute-start.8) | collective-permute-done | bytes 96 | tf_op jit(solution)/shard_map/ppermute | solution.py:270
  94.5 0.6 fusion.3
  95.6 9.0 %rows.1 = f32[2,8,64,1024]{3,2,1,0:T(8,128)} custom-call(bf16[8,1024,128]{2,1,0:T(8,128)(2,1)S(1)} %get-tuple-element.4.own, bf16[8,1024,128]{2,1,0:T(8,128)(2,1)} %collective-permute-done.7.other, bf16[4,1024,512]{2,1,0:T(8,128)(2,1)} %constant.43.clone.table), custom_call_target="tpu_custom_call" | custom-call | tf_op jit(solution)/shard_map/rows/pallas_call | solution.py:246
  (18 shorter events, 0.4 us)
Async XLA Ops:
  3.6 7.0 %collective-permute-start = (s32[56,128]{1,0:T(8,128)}, s32[56,128]{1,0:T(8,128)S(1)}, u32[]{:S(2)}, u32[]{:S(2)}) collective-permute-start(s32[56,128]{1,0:T(8,128)} %pack.1), channel_id=1, source_target_pairs={{0,2},{1,3},{2,4},{3,5},{4,6},{5,7},{6,8},{7,9},{8,10},{9,11},{10,... | collective-permute-start | bytes 86024 | tf_op jit(solution)/shard_map/ppermute | solution.py:265
  5.2 8.5 %collective-permute-start.1 = (s32[56,128]{1,0:T(8,128)}, s32[56,128]{1,0:T(8,128)S(1)}, u32[]{:S(2)}, u32[]{:S(2)}) collective-permute-start(s32[56,128]{1,0:T(8,128)} %pack.1), channel_id=1, source_target_pairs={{0,14},{1,15},{2,0},{3,1},{4,2},{5,3},{6,4},{7,5},{8,6},{9,7},{10,... | collective-permute-start | bytes 86024 | tf_op jit(solution)/shard_map/ppermute | solution.py:265
  11.4 11.8 %collective-permute-start.3 = (s32[112,128]{1,0:T(8,128)S(1)}, s32[112,128]{1,0:T(8,128)S(1)}, u32[]{:S(2)}, u32[]{:S(2)}) collective-permute-start(s32[112,128]{1,0:T(8,128)S(1)} %pad_add_fusion.1), channel_id=1, source_target_pairs={{0,10},{1,11},{2,12},{3,13},{4,14},{5,15},{6,0},{7,1},{8,2},{9,3},... | collective-permute-start | bytes 172040 | tf_op jit(solution)/shard_map/ppermute | solution.py:265
  14.5 8.6 %collective-permute-start.2 = (s32[168,128]{1,0:T(8,128)S(1)}, s32[168,128]{1,0:T(8,128)S(1)}, u32[]{:S(2)}, u32[]{:S(2)}) collective-permute-start(s32[168,128]{1,0:T(8,128)S(1)} %pad_add_fusion), channel_id=1, source_target_pairs={{0,6},{1,7},{2,8},{3,9},{4,10},{5,11},{6,12},{7,13},{8,14},{9,15},... | collective-permute-start | bytes 258056 | tf_op jit(solution)/shard_map/ppermute | solution.py:265
  23.1 5.8 %collective-permute-start.6 = (s32[448,128]{1,0:T(8,128)S(1)}, s32[448,128]{1,0:T(8,128)S(1)}, u32[]{:S(2)}, u32[]{:S(2)}) collective-permute-start(s32[448,128]{1,0:T(8,128)S(1)} %constant_dynamic-update-slice_fusion.g0), channel_id=1, source_target_pairs={{0,48},{16,64},{32,80},{48,96},{64,112},{80,128},{96,144},{112,160... | collective-permute-start | bytes 688136 | tf_op jit(solution)/shard_map/ppermute | solution.py:260
  25.7 8.7 %collective-permute-start.5 = (s32[448,128]{1,0:T(8,128)S(1)}, s32[448,128]{1,0:T(8,128)S(1)}, u32[]{:S(2)}, u32[]{:S(2)}) collective-permute-start(s32[448,128]{1,0:T(8,128)S(1)} %constant_dynamic-update-slice_fusion.g0), channel_id=1, source_target_pairs={{0,32},{16,48},{32,64},{48,80},{64,96},{80,112},{96,128},{112,144}... | collective-permute-start | bytes 688136 | tf_op jit(solution)/shard_map/ppermute | solution.py:260
  27.2 14.6 %collective-permute-start.4 = (s32[448,128]{1,0:T(8,128)S(1)}, s32[448,128]{1,0:T(8,128)S(1)}, u32[]{:S(2)}, u32[]{:S(2)}) collective-permute-start(s32[448,128]{1,0:T(8,128)S(1)} %constant_dynamic-update-slice_fusion.g0), channel_id=1, source_target_pairs={{0,16},{16,32},{32,48},{48,64},{64,80},{80,96},{96,112},{112,128},... | collective-permute-start | bytes 688136 | tf_op jit(solution)/shard_map/ppermute | solution.py:260
  90.3 5.3 %collective-permute-start.7 = (bf16[8,1024,128]{2,1,0:T(8,128)(2,1)}, bf16[8,1024,128]{2,1,0:T(8,128)(2,1)}, u32[]{:S(2)}, u32[]{:S(2)}) collective-permute-start(bf16[8,1024,128]{2,1,0:T(8,128)(2,1)} %get-tuple-element.5), channel_id=1, source_target_pairs={{0,1},{1,0},{2,3},{3,2},{4,5},{5,4},{6,7},{7,6},{8,9},{9,8},{10,11... | collective-permute-start | bytes 6291464 | tf_op jit(solution)/shard_map/ppermute | solution.py:270
  90.7 3.8 %collective-permute-start.8 = (f32[16]{0:T(128)S(1)}, f32[16]{0:T(128)S(1)}, u32[]{:S(2)}, u32[]{:S(2)}) collective-permute-start(f32[16]{0:T(128)S(1)} %convert_element_type.7), channel_id=1, source_target_pairs={{0,1},{1,0},{2,3},{3,2},{4,5},{5,4},{6,7},{7,6},{8,9},{9,8},{10,11... | collective-permute-start | bytes 200 | tf_op jit(solution)/shard_map/ppermute | solution.py:270

commit v2 on v1

--- a/solution.py
+++ b/solution.py
@@ -18,7 +18,6 @@
 BINS_DEV = 12
 SLABS = 4
 CHIPS = 8
-SOURCES = SLABS * CHIPS
 ROWS = 56
 META = 4 * BINS_DEV
 RATE = 0.08
@@ -27,8 +26,9 @@
 TOP = 32767.0
 TILES = 4
 LANES = 128
-UNROLL = 2
-ENTRIES = SOURCES * BINS_DEV + UNROLL
+UNROLL = 16
+DEPTH = NY + PATCH
+WIDTH = math.sqrt(RATE * math.log2(math.e))
 
 
 @functools.lru_cache(maxsize=None)
@@ -78,7 +78,7 @@
         meta = jnp.where(lane == 16 + b, home[0] * (NY // 16) + anchors[1, b], meta)
         meta = jnp.where(lane == 32 + b, anchors[0, b], meta)
         meta = jnp.where(lane == 48 + b, anchors[2, b], meta)
-        meta = jnp.where(lane == 64 + b, helpers[b, 0], meta)
+        meta = jnp.where(lane == 64 + b, helpers[b], meta)
         meta = jnp.where(lane == 80 + b, exponent[b : b + 1, 0:1], meta)
     out[META:ROWS, :] = jnp.broadcast_to(meta, (ROWS - META, LANES))
 
@@ -95,30 +95,10 @@
     )(counts, anchors, helpers, home, positions, forces)
 
 
-def spread_kernel(
-    core, meta, scale, g0, g1, g2, g3, table, own, other,
-    data, grid, wave, rows, offsets, ys, zs, scales,
-):
-    chunk = 64
-
-    def clear(i, carry):
-        at = pl.ds(pl.multiple_of(i * chunk, chunk), chunk)
-        zero = jnp.zeros((chunk, LANES), jnp.float32)
-        grid[0, at, :] = zero
-        grid[1, at, :] = zero
-        return carry
-
-    lax.fori_loop(0, XS * (NY + PATCH) // chunk, clear, 0)
-    for s, block in enumerate((g0, g1, g2, g3)):
-        data[s * CHIPS * ROWS : (s + 1) * CHIPS * ROWS, :] = block[...]
-    for c in range(2):
-        lanes = slice(c * LANES, (c + 1) * LANES)
-        wave[c, :NZ, :] = table[:, lanes].astype(jnp.float32)
-        wave[c, NZ:, :] = table[:PATCH, lanes].astype(jnp.float32)
+def gather_bins(meta, scale, slab, sources, lists):
+    rows, offsets, ys, zs, scales = lists
 
     def source(src, total):
-        slab = src // CHIPS
-
         def more(state):
             b, _ = state
             return jnp.logical_and(b < BINS_DEV, meta[src, jnp.minimum(b, BINS_DEV - 1)] > 0)
@@ -126,7 +106,7 @@
         def add(state):
             b, k = state
             rows[k] = src * ROWS + 4 * b
-            offsets[k] = XS * slab - meta[src, 32 + b]
+            offsets[k] = XS * (slab + src // CHIPS) - meta[src, 32 + b]
             ys[k] = meta[src, 16 + b]
             zs[k] = meta[src, 48 + b]
             scales[k] = scale[src, b]
@@ -134,34 +114,40 @@
 
         return lax.while_loop(more, add, (jnp.int32(0), total))[1]
 
-    total = lax.fori_loop(0, SOURCES, source, jnp.int32(0))
+    total = lax.fori_loop(0, sources, source, jnp.int32(0))
     for extra in range(UNROLL):
         rows[total + extra] = 0
         offsets[total + extra] = 0
         ys[total + extra] = 0
         zs[total + extra] = 0
         scales[total + extra] = jnp.float32(0.0)
-
+    return total
+
+
+def add_bins(total, lists, data, wave, grid):
+    rows, offsets, ys, zs, scales = lists
     plane = lax.broadcasted_iota(jnp.int32, (XS, LANES), 0)
-    cell = lax.broadcasted_iota(jnp.int32, (PATCH, LANES), 0).astype(jnp.float32)
+    cell = lax.broadcasted_iota(jnp.int32, (PATCH, LANES), 0).astype(jnp.float32) * WIDTH
 
     def one(k):
         row = rows[k]
         index = plane + offsets[k]
         inside = jnp.logical_and(index >= 0, index < PATCH)
-        along_x = index.astype(jnp.float32)
+        along_x = index.astype(jnp.float32) * WIDTH
         left, right = [], []
         for half in range(2):
             first = data[pl.ds(row + half, 1), :]
             second = data[pl.ds(row + 2 + half, 1), :]
-            px = (first & 0xFFFF).astype(jnp.float32) * STEP + LOW
-            py = ((first >> 16) & 0xFFFF).astype(jnp.float32) * STEP + LOW
-            pz = (second & 0xFFFF).astype(jnp.float32) * STEP + LOW
+            px = (first & 0xFFFF).astype(jnp.float32) * (STEP * WIDTH) + LOW * WIDTH
+            py = ((first >> 16) & 0xFFFF).astype(jnp.float32) * (STEP * WIDTH) + LOW * WIDTH
+            pz = (second & 0xFFFF).astype(jnp.float32) * (STEP * WIDTH) + LOW * WIDTH
             force = (second >> 16).astype(jnp.float32) * scales[k]
-            ax = jnp.where(inside, jnp.exp(-RATE * (along_x - px) ** 2) * force, 0.0)
-            ay = jnp.exp(-RATE * (cell - py) ** 2)
-            az = jnp.exp(-RATE * (cell - pz) ** 2)
-            left.append((ay[:, None, :] * ax[None, :, :]).reshape(PATCH * XS, LANES).astype(jnp.bfloat16))
+            dx, dy, dz = along_x - px, cell - py, cell - pz
+            ax = jnp.where(inside, jnp.exp2(-(dx * dx)) * force, 0.0)
+            ay = jnp.exp2(-(dy * dy))
+            az = jnp.exp2(-(dz * dz))
+            products = [ay * ax[x : x + 1, :] for x in range(XS)]
+            left.append(jnp.concatenate(products, axis=0).astype(jnp.bfloat16))
             right.append(az.astype(jnp.bfloat16))
         patch = lax.dot_general(
             jnp.concatenate(left, axis=1),
@@ -175,53 +161,93 @@
     def several(i, carry):
         found = [one(UNROLL * i + u) for u in range(UNROLL)]
         for u in range(UNROLL):
-            at = pl.ds(pl.multiple_of(ys[UNROLL * i + u] * XS, XS), PATCH * XS)
-            grid[0, at, :] += found[u][:, :LANES]
-            grid[1, at, :] += found[u][:, LANES:]
+            y = ys[UNROLL * i + u]
+            for c in range(2):
+                for x in range(XS):
+                    at = pl.ds((c * XS + x) * DEPTH + y, PATCH)
+                    grid[at, :] += found[u][x * PATCH : (x + 1) * PATCH, c * LANES : (c + 1) * LANES]
         return carry
 
     lax.fori_loop(0, (total + UNROLL - 1) // UNROLL, several, 0)
-    grid[0, : PATCH * XS, :] += grid[0, NY * XS :, :]
-    grid[1, : PATCH * XS, :] += grid[1, NY * XS :, :]
-    mine = core[1]
+
+def near_kernel(chip, meta, scale, block, table, grid, wave, *lists):
+    def clear(i, carry):
+        at = pl.ds(pl.multiple_of(i * DEPTH, XS), DEPTH)
+        grid[at, :] = jnp.zeros((DEPTH, LANES), jnp.float32)
+        return carry
+
+    lax.fori_loop(0, 2 * XS, clear, 0)
+    for c in range(2):
+        lanes = slice(c * LANES, (c + 1) * LANES)
+        wave[c, :NZ, :] = table[:, lanes].astype(jnp.float32)
+        wave[c, NZ:, :] = table[:PATCH, lanes].astype(jnp.float32)
+    total = gather_bins(meta, scale, 0, CHIPS, lists)
+    add_bins(total, lists, block, wave, grid)
+
+
+def far_kernel(core, meta, scale, g1, g2, g3, wave, grid_in, own, other, grid, data, *lists):
+    for s, block in enumerate((g1, g2, g3)):
+        data[s * CHIPS * ROWS : (s + 1) * CHIPS * ROWS, :] = block[...]
+    total = gather_bins(meta, scale, 1, (SLABS - 1) * CHIPS, lists)
+    add_bins(total, lists, data, wave, grid)
+    mine = core[0]
 
     def finish(i, carry):
-        for x in range(XS):
-            at = pl.ds(i * chunk * XS + x, chunk, stride=XS)
-            to = pl.ds(pl.multiple_of(i * chunk, chunk), chunk)
-            own[x, to, :] = grid[mine, at, :].astype(jnp.bfloat16)
-            other[x, to, :] = grid[1 - mine, at, :].astype(jnp.bfloat16)
+        for c, half in ((mine, own), (1 - mine, other)):
+            start = pl.multiple_of((c * XS + i) * DEPTH, XS)
+            grid[pl.ds(start, PATCH), :] += grid[pl.ds(start + NY, PATCH), :]
+            half[i] = grid[pl.ds(start, NY), :].astype(jnp.bfloat16)
         return carry
 
-    lax.fori_loop(0, NY // chunk, finish, 0)
-
-
-def spread(core, meta, scale, blocks, z_table):
+    lax.fori_loop(0, XS, finish, 0)
+
+
+def bin_lists(sources):
+    entries = sources * BINS_DEV + UNROLL
+    return [pltpu.SMEM((entries,), jnp.int32)] * 4 + [pltpu.SMEM((entries,), jnp.float32)]
+
+
+def spread_near(chip, meta, scale, block, z_table):
     smem = pl.BlockSpec(memory_space=pltpu.SMEM)
     vmem = pl.BlockSpec(memory_space=pltpu.VMEM)
-    half = jax.ShapeDtypeStruct((XS, NY, LANES), jnp.bfloat16)
     return pl.pallas_call(
-        spread_kernel,
-        out_shape=(half, half),
+        near_kernel,
+        out_shape=(
+            pltpu.VMEM((2 * XS * DEPTH, LANES), jnp.float32),
+            pltpu.VMEM((2, DEPTH, LANES), jnp.float32),
+        ),
         grid_spec=pltpu.PrefetchScalarGridSpec(
             num_scalar_prefetch=3,
             grid=(1,),
-            in_specs=[vmem] * 4 + [pl.BlockSpec((None, NZ, 2 * LANES), lambda i, core, meta, scale: (core[0], 0, 0))],
+            in_specs=[vmem, pl.BlockSpec((None, NZ, 2 * LANES), lambda i, chip, meta, scale: (chip[0], 0, 0))],
             out_specs=[vmem, vmem],
-            scratch_shapes=[
-                pltpu.VMEM((SOURCES * ROWS, LANES), jnp.int32),
-                pltpu.VMEM((2, XS * (NY + PATCH), LANES), jnp.float32),
-                pltpu.VMEM((2, NZ + PATCH, LANES), jnp.float32),
-                pltpu.SMEM((ENTRIES,), jnp.int32),
-                pltpu.SMEM((ENTRIES,), jnp.int32),
-                pltpu.SMEM((ENTRIES,), jnp.int32),
-                pltpu.SMEM((ENTRIES,), jnp.int32),
-                pltpu.SMEM((ENTRIES,), jnp.float32),
-            ],
+            scratch_shapes=bin_lists(CHIPS),
         ),
-        compiler_params=pltpu.CompilerParams(vmem_limit_bytes=48 * 2**20),
-        name="spread",
-    )(core, meta, scale, *blocks, z_table)
+        compiler_params=pltpu.CompilerParams(vmem_limit_bytes=24 * 2**20),
+        cost_estimate=pl.CostEstimate(flops=2**32, bytes_accessed=2**23, transcendentals=2**20),
+        name="near",
+    )(chip, meta, scale, block, z_table)
+
+
+def spread_far(core, meta, scale, blocks, wave, grid):
+    smem = pl.BlockSpec(memory_space=pltpu.SMEM)
+    vmem = pl.BlockSpec(memory_space=pltpu.VMEM)
+    half = (XS, NY, LANES)
+    sources = (SLABS - 1) * CHIPS
+    return pl.pallas_call(
+        far_kernel,
+        out_shape=(
+            pltpu.VMEM(half, jnp.bfloat16),
+            jax.ShapeDtypeStruct(half, jnp.bfloat16),
+            pltpu.VMEM((2 * XS * DEPTH, LANES), jnp.float32),
+        ),
+        in_specs=[smem] * 3 + [vmem] * 5,
+        out_specs=[vmem] * 3,
+        input_output_aliases={7: 2},
+        scratch_shapes=[pltpu.VMEM((sources * ROWS, LANES), jnp.int32)] + bin_lists(sources),
+        compiler_params=pltpu.CompilerParams(vmem_limit_bytes=24 * 2**20),
+        name="far",
+    )(core, meta, scale, *blocks, wave, grid)
 
 
 def rows_kernel(own, other, table, out, lines):
@@ -277,22 +303,27 @@
     return jnp.concatenate([near, before, after], axis=0)
 
 
+def powers(meta):
+    return jnp.exp2(meta[:, 80:96].astype(jnp.float32)) * (1.0 / TOP)
+
+
 def body(positions, forces, counts, anchors, helpers):
     z_table, y_table = tables()
     home = lax.axis_index("narrow").astype(jnp.int32)
-    packed = pack(positions, forces, counts, anchors, helpers, home.reshape(1))
+    packed = pack(positions, forces, counts, anchors, helpers.reshape(BINS_DEV), home.reshape(1))
     block = ring(packed)
-    blocks = [block] + [slab_shift(block, d) for d in range(1, SLABS)]
-    meta = jnp.concatenate([g.reshape(CHIPS, ROWS, LANES)[:, META] for g in blocks], axis=0)
-    scale = jnp.exp2(meta[:, 80:96].astype(jnp.float32)) * (1.0 / TOP)
-    numbers, choice = meta[:CHIPS, :BINS_DEV], meta[:CHIPS, 64 : 64 + BINS_DEV]
+    blocks = [slab_shift(block, d) for d in range(1, SLABS)]
+    here = block.reshape(CHIPS, ROWS, LANES)[:, META]
+    numbers, choice = here[:, :BINS_DEV], here[:, 64 : 64 + BINS_DEV]
     helper_index = jnp.arange(16, dtype=jnp.int32)
     matches = choice[:, :, None] == helper_index[None, None, :]
     load = jnp.sum(jnp.where(matches, numbers[:, :, None], 0), axis=(0, 1)).astype(jnp.float32)
     load = load + partner(load)
+    grid, wave = spread_near((home // 2).reshape(1), here, powers(here), block, pltpu.with_memory_space_constraint(jnp.asarray(z_table), pltpu.HBM))
+    wave, load = lax.optimization_barrier((wave, load))
     helper_load = (jnp.sum(jnp.where(helper_index == home, load, 0.0)) / BIN).reshape(1, 1)
-    core = jnp.stack([home // 2, home % 2])
-    own, other = spread(core, meta, scale, blocks, jnp.asarray(z_table))
+    meta = jnp.concatenate([g.reshape(CHIPS, ROWS, LANES)[:, META] for g in blocks], axis=0)
+    own, other, _ = spread_far((home % 2).reshape(1), meta, powers(meta), blocks, wave, grid)
     spectrum = along_rows(own, partner(other), jnp.asarray(y_table))
     return (spectrum, helper_load)
 

time: 105 us -> 72.6 us (0.69)
  the two profiles are of different devices: /device:TPU:9 before, /device:TPU:1 now
where the time goes in v2:
time: 72.6 us; the launch traced here: 71.5 us
  Pallas kernels  30.4 us (42%)
  waiting for transfers between devices  17.7 us (24%)
  starting transfers between devices  17.4 us (24%)
  between operations  2.54 us (3%)
  other arithmetic  2.45 us (3%)
  local copies, waits for them, and re-layouts  1.02 us (1%)
    pallas_call x1, Pallas kernels, spread_far(): pl.pallas_call(far_kernel, out_shape=(pltpu.VMEM(half, jnp.bfloat16), jax...  14.3 us
    ppermute x4, starting transfers between devices, chip_shift(): lax.ppermute(block, 'narrow', [(i, (i + 2 * distance) % count) for i in r...  9.94 us
    pallas_call x1, Pallas kernels, along_rows(): pl.pallas_call(rows_kernel, out_shape=jax.ShapeDtypeStruct((2, XS, 64, NY...  8.94 us
    ppermute x4, waiting for transfers between devices, chip_shift(): lax.ppermute(block, 'narrow', [(i, (i + 2 * distance) % count) for i in r...  8.16 us
    ppermute x3, waiting for transfers between devices, slab_shift(): lax.ppermute(block, 'wide', [(i, (i + distance) % count) for i in range(c...  6.36 us
    pallas_call x1, Pallas kernels, spread_near(): pl.pallas_call(near_kernel, out_shape=(pltpu.VMEM((2 * XS * DEPTH, LANES)...  5.62 us
    ppermute x3, starting transfers between devices, slab_shift(): lax.ppermute(block, 'wide', [(i, (i + distance) % count) for i in range(c...  4.62 us
    ppermute x2, waiting for transfers between devices, partner(): return lax.ppermute(block, 'narrow', [(i, i ^ 1) for i in range(count)])  3.15 us
  transfers between devices with their start and end apart: 9, of which 4 were waited for; matrix products, arithmetic and copies ran while one was open for 5% of the time, Pallas kernels for 8%

profile of v2, /device:TPU:1, one launch (start us, length us, event | category | flops | bytes accessed | tf_op | source)
XLA Modules:
  0.0 71.5 jit_solution(778985759743878911)
XLA Ops:
  0.6 1.6 %pack.1 = s32[56,128]{1,0:T(8,128)} custom-call(s32[12]{0:T(128)} %counts.1, s32[3,12]{1,0:T(4,128)} %anchors.1, s32[12]{0:T(128)} %bitcast.31, s32[1]{0:T(128)} %bitcast.2.home, f32[12,3,256]{2,1,0:T(4,128)} %positions.1, f32[12,256]{1,0:T(8,128)} %forces.1), custom_call_target="tpu_custom_call" | custom-call | tf_op jit(solution)/shard_map/pack/pallas_call | solution.py:89
  2.2 2.5 %collective-permute-start = (s32[56,128]{1,0:T(8,128)}, s32[56,128]{1,0:T(8,128)S(1)}, u32[]{:S(2)}, u32[]{:S(2)}) collective-permute-start(s32[56,128]{1,0:T(8,128)} %pack.1), channel_id=1, source_target_pairs={{0,2},{1,3},{2,4},{3,5},{4,6},{5,7},{6,8},{7,9},{8,10},{9,11},{10,... | collective-permute-start | bytes 86024 | tf_op jit(solution)/shard_map/ppermute | solution.py:291
  4.7 3.9 %collective-permute-start.1 = (s32[56,128]{1,0:T(8,128)}, s32[56,128]{1,0:T(8,128)S(1)}, u32[]{:S(2)}, u32[]{:S(2)}) collective-permute-start(s32[56,128]{1,0:T(8,128)} %pack.1), channel_id=1, source_target_pairs={{0,14},{1,15},{2,0},{3,1},{4,2},{5,3},{6,4},{7,5},{8,6},{9,7},{10,... | collective-permute-start | bytes 86024 | tf_op jit(solution)/shard_map/ppermute | solution.py:291
  8.6 1.5 %collective-permute-done = s32[56,128]{1,0:T(8,128)S(1)} collective-permute-done((s32[56,128]{1,0:T(8,128)}, s32[56,128]{1,0:T(8,128)S(1)}, u32[]{:S(2)}, u32[]{:S(2)}) %collective-permute-start) | collective-permute-done | bytes 28704 | tf_op jit(solution)/shard_map/ppermute | solution.py:291
  10.1 0.8 %pad_add_fusion.1 = s32[112,128]{1,0:T(8,128)S(1)} fusion(s32[56,128]{1,0:T(8,128)} %pack.1, s32[56,128]{1,0:T(8,128)S(1)} %collective-permute-done), kind=kLoop, calls=%fused_computation.1 | loop fusion | flops 14336 | bytes 114688 | tf_op jit(solution)/shard_map/concatenate | solution.py:300
  10.8 2.4 %collective-permute-start.3 = (s32[112,128]{1,0:T(8,128)S(1)}, s32[112,128]{1,0:T(8,128)S(1)}, u32[]{:S(2)}, u32[]{:S(2)}) collective-permute-start(s32[112,128]{1,0:T(8,128)S(1)} %pad_add_fusion.1), channel_id=1, source_target_pairs={{0,10},{1,11},{2,12},{3,13},{4,14},{5,15},{6,0},{7,1},{8,2},{9,3},... | collective-permute-start | bytes 172040 | tf_op jit(solution)/shard_map/ppermute | solution.py:291
  13.2 0.8 %pad_add_fusion = s32[168,128]{1,0:T(8,128)S(1)} fusion(s32[56,128]{1,0:T(8,128)S(1)} %collective-permute-done.1, s32[56,128]{1,0:T(8,128)} %pack.1, s32[56,128]{1,0:T(8,128)S(1)} %collective-permute-done), kind=kLoop, calls=%fused_computation | loop fusion | flops 43008 | bytes 172032 | tf_op jit(solution)/shard_map/concatenate | solution.py:300
  13.9 1.2 %collective-permute-start.2 = (s32[168,128]{1,0:T(8,128)S(1)}, s32[168,128]{1,0:T(8,128)S(1)}, u32[]{:S(2)}, u32[]{:S(2)}) collective-permute-start(s32[168,128]{1,0:T(8,128)S(1)} %pad_add_fusion), channel_id=1, source_target_pairs={{0,6},{1,7},{2,8},{3,9},{4,10},{5,11},{6,12},{7,13},{8,14},{9,15},... | collective-permute-start | bytes 258056 | tf_op jit(solution)/shard_map/ppermute | solution.py:291
  15.1 0.8 %constant_dynamic-update-slice_fusion.3 = s32[448,128]{1,0:T(8,128)S(1)} fusion(s32[448,128]{1,0:T(8,128)S(1)} %constant_dynamic-update-slice_fusion.4, s32[56,128]{1,0:T(8,128)} %pack.1), kind=kLoop, calls=%fused_computation.12 | loop fusion | bytes 57344
  15.9 6.7 %collective-permute-done.2 = s32[168,128]{1,0:T(8,128)S(1)} collective-permute-done((s32[168,128]{1,0:T(8,128)S(1)}, s32[168,128]{1,0:T(8,128)S(1)}, u32[]{:S(2)}, u32[]{:S(2)}) %collective-permute-start.2) | collective-permute-done | bytes 86048 | tf_op jit(solution)/shard_map/ppermute | solution.py:291
  22.8 2.5 %collective-permute-start.6 = (s32[448,128]{1,0:T(8,128)S(1)}, s32[448,128]{1,0:T(8,128)S(1)}, u32[]{:S(2)}, u32[]{:S(2)}) collective-permute-start(s32[448,128]{1,0:T(8,128)S(1)} %constant_dynamic-update-slice_fusion.block), channel_id=1, source_target_pairs={{0,48},{16,64},{32,80},{48,96},{64,112},{80,128},{96,144},{112,160... | collective-permute-start | bytes 688136 | tf_op jit(solution)/shard_map/ppermute | solution.py:286
  25.2 1.5 %collective-permute-start.5 = (s32[448,128]{1,0:T(8,128)S(1)}, s32[448,128]{1,0:T(8,128)S(1)}, u32[]{:S(2)}, u32[]{:S(2)}) collective-permute-start(s32[448,128]{1,0:T(8,128)S(1)} %constant_dynamic-update-slice_fusion.block), channel_id=1, source_target_pairs={{0,32},{16,48},{32,64},{48,80},{64,96},{80,112},{96,128},{112,144}... | collective-permute-start | bytes 688136 | tf_op jit(solution)/shard_map/ppermute | solution.py:286
  26.8 0.6 collective-permute-start.4
  27.4 0.1 copy.18
  27.5 0.1 copy.19
  27.6 0.1 select_reduce_fusion
  27.7 2.9 %collective-permute-start.7 = (f32[16]{0:T(128)S(1)}, f32[16]{0:T(128)S(1)}, u32[]{:S(2)}, u32[]{:S(2)}) collective-permute-start(f32[16]{0:T(128)S(1)} %convert_element_type.11), channel_id=1, source_target_pairs={{0,1},{1,0},{2,3},{3,2},{4,5},{5,4},{6,7},{7,6},{8,9},{9,8},{10,11... | collective-permute-start | bytes 200 | tf_op jit(solution)/shard_map/ppermute | solution.py:296
  30.6 5.6 %near.1 = (f32[16768,128]{1,0:T(8,128)S(1)}, f32[2,1048,128]{2,1,0:T(8,128)S(1)}) custom-call(s32[1]{0:T(128)} %bitcast.9.chip, s32[8,128]{1,0:T(8,128)S(1)} %bitcast.26, f32[8,16]{1,0:T(8,128)S(1)} %exponential_multiply_fusion.scale, s32[448,128]{1,0:T(8,128)S(1)} %constant_dynamic-update-slice_fusion.block, bf16[8,1024,256]{2,1,0:T(8,128)(2,1)} %constant.44.clone.table), custom_call_target="tpu_custom_call" | custom-call | flops 4294967296 | bytes 8388608 | tf_op jit(solution)/shard_map/near/pallas_call | solution.py:213
  36.2 6.4 %collective-permute-done.4.g1 = s32[448,128]{1,0:T(8,128)S(1)} collective-permute-done((s32[448,128]{1,0:T(8,128)S(1)}, s32[448,128]{1,0:T(8,128)S(1)}, u32[]{:S(2)}, u32[]{:S(2)}) %collective-permute-start.4) | collective-permute-done | bytes 229408 | tf_op jit(solution)/shard_map/ppermute | solution.py:286
  42.6 0.1 fusion.2.scale
  42.7 14.3 %far.1 = (bf16[8,1024,128]{2,1,0:T(8,128)(2,1)S(1)}, bf16[8,1024,128]{2,1,0:T(8,128)(2,1)}, f32[16768,128]{1,0:T(8,128)S(1)}) custom-call(s32[1]{0:T(128)} %bitcast.core, s32[24,128]{1,0:T(8,128)S(1)} %pad_add_fusion.2.meta, f32[24,16]{1,0:T(8,128)S(1)} %fusion.2.scale, s32[448,128]{1,0:T(8,128)S(1)} %collective-permute-done.4.g1, ...), custom_call_target="tpu_custom_call", output_to_operand_aliasing={{2}: (7, {})} | custom-call | tf_op jit(solution)/shard_map/far/pallas_call | solution.py:237
  57.0 0.7 fusion.3
  58.3 3.1 %collective-permute-done.8.other = bf16[8,1024,128]{2,1,0:T(8,128)(2,1)} collective-permute-done((bf16[8,1024,128]{2,1,0:T(8,128)(2,1)}, bf16[8,1024,128]{2,1,0:T(8,128)(2,1)}, u32[]{:S(2)}, u32[]{:S(2)}) %collective-permute-start.8) | collective-permute-done | bytes 2097184 | tf_op jit(solution)/shard_map/ppermute | solution.py:296
  61.5 8.9 %rows.1 = f32[2,8,64,1024]{3,2,1,0:T(8,128)} custom-call(bf16[8,1024,128]{2,1,0:T(8,128)(2,1)S(1)} %get-tuple-element.11.own, bf16[8,1024,128]{2,1,0:T(8,128)(2,1)} %collective-permute-done.8.other, bf16[4,1024,512]{2,1,0:T(8,128)(2,1)} %constant.45.clone.table), custom_call_target="tpu_custom_call" | custom-call | tf_op jit(solution)/shard_map/rows/pallas_call | solution.py:272
  (19 shorter events, 0.2 us)
Async XLA Ops:
  2.2 7.9 %collective-permute-start = (s32[56,128]{1,0:T(8,128)}, s32[56,128]{1,0:T(8,128)S(1)}, u32[]{:S(2)}, u32[]{:S(2)}) collective-permute-start(s32[56,128]{1,0:T(8,128)} %pack.1), channel_id=1, source_target_pairs={{0,2},{1,3},{2,4},{3,5},{4,6},{5,7},{6,8},{7,9},{8,10},{9,11},{10,... | collective-permute-start | bytes 86024 | tf_op jit(solution)/shard_map/ppermute | solution.py:291
  4.7 8.5 %collective-permute-start.1 = (s32[56,128]{1,0:T(8,128)}, s32[56,128]{1,0:T(8,128)S(1)}, u32[]{:S(2)}, u32[]{:S(2)}) collective-permute-start(s32[56,128]{1,0:T(8,128)} %pack.1), channel_id=1, source_target_pairs={{0,14},{1,15},{2,0},{3,1},{4,2},{5,3},{6,4},{7,5},{8,6},{9,7},{10,... | collective-permute-start | bytes 86024 | tf_op jit(solution)/shard_map/ppermute | solution.py:291
  10.8 11.8 %collective-permute-start.3 = (s32[112,128]{1,0:T(8,128)S(1)}, s32[112,128]{1,0:T(8,128)S(1)}, u32[]{:S(2)}, u32[]{:S(2)}) collective-permute-start(s32[112,128]{1,0:T(8,128)S(1)} %pad_add_fusion.1), channel_id=1, source_target_pairs={{0,10},{1,11},{2,12},{3,13},{4,14},{5,15},{6,0},{7,1},{8,2},{9,3},... | collective-permute-start | bytes 172040 | tf_op jit(solution)/shard_map/ppermute | solution.py:291
  13.9 8.6 %collective-permute-start.2 = (s32[168,128]{1,0:T(8,128)S(1)}, s32[168,128]{1,0:T(8,128)S(1)}, u32[]{:S(2)}, u32[]{:S(2)}) collective-permute-start(s32[168,128]{1,0:T(8,128)S(1)} %pad_add_fusion), channel_id=1, source_target_pairs={{0,6},{1,7},{2,8},{3,9},{4,10},{5,11},{6,12},{7,13},{8,14},{9,15},... | collective-permute-start | bytes 258056 | tf_op jit(solution)/shard_map/ppermute | solution.py:291
  22.8 13.4 %collective-permute-start.6 = (s32[448,128]{1,0:T(8,128)S(1)}, s32[448,128]{1,0:T(8,128)S(1)}, u32[]{:S(2)}, u32[]{:S(2)}) collective-permute-start(s32[448,128]{1,0:T(8,128)S(1)} %constant_dynamic-update-slice_fusion.block), channel_id=1, source_target_pairs={{0,48},{16,64},{32,80},{48,96},{64,112},{80,128},{96,144},{112,160... | collective-permute-start | bytes 688136 | tf_op jit(solution)/shard_map/ppermute | solution.py:286
  25.2 11.0 %collective-permute-start.5 = (s32[448,128]{1,0:T(8,128)S(1)}, s32[448,128]{1,0:T(8,128)S(1)}, u32[]{:S(2)}, u32[]{:S(2)}) collective-permute-start(s32[448,128]{1,0:T(8,128)S(1)} %constant_dynamic-update-slice_fusion.block), channel_id=1, source_target_pairs={{0,32},{16,48},{32,64},{48,80},{64,96},{80,112},{96,128},{112,144}... | collective-permute-start | bytes 688136 | tf_op jit(solution)/shard_map/ppermute | solution.py:286
  26.8 15.8 %collective-permute-start.4 = (s32[448,128]{1,0:T(8,128)S(1)}, s32[448,128]{1,0:T(8,128)S(1)}, u32[]{:S(2)}, u32[]{:S(2)}) collective-permute-start(s32[448,128]{1,0:T(8,128)S(1)} %constant_dynamic-update-slice_fusion.block), channel_id=1, source_target_pairs={{0,16},{16,32},{32,48},{48,64},{64,80},{80,96},{96,112},{112,128},... | collective-permute-start | bytes 688136 | tf_op jit(solution)/shard_map/ppermute | solution.py:286
  27.7 8.5 %collective-permute-start.7 = (f32[16]{0:T(128)S(1)}, f32[16]{0:T(128)S(1)}, u32[]{:S(2)}, u32[]{:S(2)}) collective-permute-start(f32[16]{0:T(128)S(1)} %convert_element_type.11), channel_id=1, source_target_pairs={{0,1},{1,0},{2,3},{3,2},{4,5},{5,4},{6,7},{7,6},{8,9},{9,8},{10,11... | collective-permute-start | bytes 200 | tf_op jit(solution)/shard_map/ppermute | solution.py:296
  57.0 4.5 %collective-permute-start.8 = (bf16[8,1024,128]{2,1,0:T(8,128)(2,1)}, bf16[8,1024,128]{2,1,0:T(8,128)(2,1)}, u32[]{:S(2)}, u32[]{:S(2)}) collective-permute-start(bf16[8,1024,128]{2,1,0:T(8,128)(2,1)} %get-tuple-element.12), channel_id=1, source_target_pairs={{0,1},{1,0},{2,3},{3,2},{4,5},{5,4},{6,7},{7,6},{8,9},{9,8},{10,11... | collective-permute-start | bytes 6291464 | tf_op jit(solution)/shard_map/ppermute | solution.py:296

commit v3 on v2

v3 whole, which is shorter than its diff:
```python
import functools
import math

import jax
import jax.numpy as jnp
import ml_dtypes
import numpy as np
from jax import lax
from jax.experimental import pallas as pl
from jax.experimental.pallas import tpu as pltpu
from jax.sharding import PartitionSpec as P

XS = 8
NY = 1024
NZ = 1024
PATCH = 24
BIN = 256
BINS_DEV = 12
SLABS = 4
CHIPS = 8
ROWS = 56
META = 4 * BINS_DEV
RATE = 0.08
LOW = 6.0
STEP = 12.0 / 65535.0
TOP = 32767.0
TILES = 1
PLANES = 2
LANES = 128
UNROLL = 16
DEPTH = NY + PATCH
WIDTH = math.sqrt(RATE * math.log2(math.e))


@functools.lru_cache(maxsize=None)
def tables():
    ordinal = np.arange(NZ)
    phase = ordinal[:, None] * ordinal[None, :] % NZ
    angle = phase.astype(np.float64) * (2.0 * math.pi / NZ)
    cos = (np.cos(angle) / math.sqrt(NZ)).astype(ml_dtypes.bfloat16)
    sin = (np.sin(angle) / math.sqrt(NZ)).astype(ml_dtypes.bfloat16)
    cz = cos.reshape(NZ, 64, 16).transpose(2, 0, 1)
    sz = sin.reshape(NZ, 64, 16).transpose(2, 0, 1)
    both = np.concatenate([cz, -sz], axis=2)
    z_table = both.reshape(CHIPS, 2, NZ, LANES).transpose(0, 2, 1, 3).reshape(CHIPS, NZ, 2 * LANES)
    y_table = np.stack([cos, sin])
    return np.ascontiguousarray(z_table), np.ascontiguousarray(y_table)


def pack_kernel(counts, anchors, helpers, home, positions, forces, out):
    bins = lax.broadcasted_iota(jnp.int32, (BINS_DEV, BIN), 0)
    slot = lax.broadcasted_iota(jnp.int32, (BINS_DEV, BIN), 1)
    limit = jnp.zeros((BINS_DEV, BIN), jnp.int32)
    for b in range(BINS_DEV):
        limit = jnp.where(bins == b, counts[b], limit)
    live = jnp.where(slot < limit, forces[...], 0.0)
    largest = jnp.max(jnp.abs(live), axis=1, keepdims=True)
    power = jnp.clip(jnp.ceil(jnp.log(largest) * (1.0 / math.log(2.0))), -126.0, 1.0)
    scaled = live * jnp.exp2(-power) * TOP
    code = jnp.clip(jnp.floor(scaled + 0.5), -TOP, TOP).astype(jnp.int32)
    exponent = power.astype(jnp.int32)
    lane = lax.broadcasted_iota(jnp.int32, (1, LANES), 1)
    meta = jnp.zeros((1, LANES), jnp.int32)
    for b in range(BINS_DEV):
        place = jnp.clip((positions[b] - LOW) * (1.0 / STEP) + 0.5, 0.0, 65535.0).astype(jnp.int32)
        first = place[0:1] | (place[1:2] << 16)
        second = place[2:3] | (code[b : b + 1] << 16)
        out[4 * b : 4 * b + 1, :] = first[:, :LANES]
        out[4 * b + 1 : 4 * b + 2, :] = first[:, LANES:]
        out[4 * b + 2 : 4 * b + 3, :] = second[:, :LANES]
        out[4 * b + 3 : 4 * b + 4, :] = second[:, LANES:]
        meta = jnp.where(lane == b, counts[b], meta)
        meta = jnp.where(lane == 16 + b, home[0] * (NY // 16) + anchors[1, b], meta)
        meta = jnp.where(lane == 32 + b, anchors[0, b], meta)
        meta = jnp.where(lane == 48 + b, anchors[2, b], meta)
        meta = jnp.where(lane == 64 + b, helpers[b], meta)
        meta = jnp.where(lane == 80 + b, exponent[b : b + 1, 0:1], meta)
    out[META:ROWS, :] = jnp.broadcast_to(meta, (ROWS - META, LANES))


def pack(positions, forces, counts, anchors, helpers, home):
    smem = pl.BlockSpec(memory_space=pltpu.SMEM)
    vmem = pl.BlockSpec(memory_space=pltpu.VMEM)
    return pl.pallas_call(
        pack_kernel,
        out_shape=jax.ShapeDtypeStruct((ROWS, LANES), jnp.int32),
        in_specs=[smem, smem, smem, smem, vmem, vmem],
        out_specs=vmem,
        name="pack",
    )(counts, anchors, helpers, home, positions, forces)


def gather_bins(metas, slab, lists):
    rows, offsets, ys, zs, powers = lists
    total = jnp.int32(0)
    for s, meta in enumerate(metas):

        def source(src, total, meta=meta, s=s):
            def more(state):
                b, _ = state
                return jnp.logical_and(b < BINS_DEV, meta[src, jnp.minimum(b, BINS_DEV - 1)] > 0)

            def add(state):
                b, k = state
                rows[k] = (s * CHIPS + src) * ROWS + 4 * b
                offsets[k] = XS * (slab + s) - meta[src, 32 + b]
                ys[k] = meta[src, 16 + b]
                zs[k] = meta[src, 48 + b]
                powers[k] = meta[src, 80 + b]
                return b + 1, k + 1

            return lax.while_loop(more, add, (jnp.int32(0), total))[1]

        total = lax.fori_loop(0, CHIPS, source, total)
    for extra in range(UNROLL):
        rows[total + extra] = 0
        offsets[total + extra] = 0
        ys[total + extra] = 0
        zs[total + extra] = 0
        powers[total + extra] = -1000
    return total


def add_bins(total, lists, data, wave, grid):
    rows, offsets, ys, zs, powers = lists
    plane = lax.broadcasted_iota(jnp.int32, (XS, LANES), 0)
    cell = lax.broadcasted_iota(jnp.int32, (PATCH, LANES), 0).astype(jnp.float32) * WIDTH

    def one(k):
        row = rows[k]
        index = plane + offsets[k]
        inside = jnp.logical_and(index >= 0, index < PATCH)
        along_x = index.astype(jnp.float32) * WIDTH
        scale = jnp.exp2(jnp.full((1, LANES), powers[k], jnp.int32).astype(jnp.float32)) * (1.0 / TOP)
        left, right = [], []
        for half in range(2):
            first = data[pl.ds(row + half, 1), :]
            second = data[pl.ds(row + 2 + half, 1), :]
            px = (first & 0xFFFF).astype(jnp.float32) * (STEP * WIDTH) + LOW * WIDTH
            py = ((first >> 16) & 0xFFFF).astype(jnp.float32) * (STEP * WIDTH) + LOW * WIDTH
            pz = (second & 0xFFFF).astype(jnp.float32) * (STEP * WIDTH) + LOW * WIDTH
            force = (second >> 16).astype(jnp.float32) * scale
            dx, dy, dz = along_x - px, cell - py, cell - pz
            ax = jnp.where(inside, jnp.exp2(-(dx * dx)) * force, 0.0)
            ay = jnp.exp2(-(dy * dy))
            az = jnp.exp2(-(dz * dz))
            products = [ay * ax[x : x + 1, :] for x in range(XS)]
            left.append(jnp.concatenate(products, axis=0).astype(jnp.bfloat16))
            right.append(az.astype(jnp.bfloat16))
        patch = lax.dot_general(
            jnp.concatenate(left, axis=1),
            jnp.concatenate(right, axis=1),
            (((1,), (1,)), ((), ())),
            preferred_element_type=jnp.float32,
        ).astype(jnp.bfloat16)
        turn = jnp.concatenate([wave[c, pl.ds(zs[k], PATCH), :] for c in range(2)], axis=1)
        return jnp.dot(patch, turn.astype(jnp.bfloat16), preferred_element_type=jnp.float32)

    def several(i, carry):
        found = [one(UNROLL * i + u) for u in range(UNROLL)]
        for u in range(UNROLL):
            y = ys[UNROLL * i + u]
            for c in range(2):
                for x in range(XS):
                    at = pl.ds((c * XS + x) * DEPTH + y, PATCH)
                    grid[at, :] += found[u][x * PATCH : (x + 1) * PATCH, c * LANES : (c + 1) * LANES]
        return carry

    lax.fori_loop(0, (total + UNROLL - 1) // UNROLL, several, 0)

def near_kernel(chip, meta, block, table, grid, wave, load, *lists):
    def clear(i, carry):
        at = pl.ds(pl.multiple_of(i * DEPTH, XS), DEPTH)
        grid[at, :] = jnp.zeros((DEPTH, LANES), jnp.float32)
        return carry

    lax.fori_loop(0, 2 * XS, clear, 0)
    for c in range(2):
        lanes = slice(c * LANES, (c + 1) * LANES)
        wave[c, :NZ, :] = table[:, lanes].astype(jnp.float32)
        wave[c, NZ:, :] = table[:PATCH, lanes].astype(jnp.float32)
    lane = lax.broadcasted_iota(jnp.int32, (1, LANES), 1)
    count = jnp.zeros((1, LANES), jnp.int32)
    for src in range(CHIPS):
        row = block[src * ROWS + META : src * ROWS + META + 1, :]
        for b in range(BINS_DEV):
            count += jnp.where(lane == row[:, 64 + b : 65 + b], row[:, b : b + 1], 0)
    load[...] = jnp.broadcast_to(count, (8, LANES))
    total = gather_bins((meta,), 0, lists)
    add_bins(total, lists, block, wave, grid)


def far_kernel(core, m1, m2, m3, g1, g2, g3, wave, load, grid_in, own, other, grid, data, *lists):
    for s, block in enumerate((g1, g2, g3)):
        data[s * CHIPS * ROWS : (s + 1) * CHIPS * ROWS, :] = block[...]
    total = gather_bins((m1, m2, m3), 1, lists)
    add_bins(total, lists, data, wave, grid)
    mine = core[0]

    def finish(i, carry):
        for c, half in ((mine, own), (1 - mine, other)):
            start = pl.multiple_of((c * XS + i) * DEPTH, XS)
            grid[pl.ds(start, PATCH), :] += grid[pl.ds(start + NY, PATCH), :]
            half[pl.ds(pl.multiple_of(i * NY, NY), NY), :] = grid[pl.ds(start, NY), :].astype(jnp.bfloat16)
        return carry

    lax.fori_loop(0, XS, finish, 0)
    row = lax.broadcasted_iota(jnp.int32, (16, LANES), 0)
    count = jnp.concatenate([load[...], load[...]], axis=0)
    tail = jnp.where(row == 0, count >> 8, jnp.where(row == 1, count & 255, 0))
    other[XS * NY :, :] = tail.astype(jnp.float32).astype(jnp.bfloat16)


def bin_lists(slabs):
    return [pltpu.SMEM((slabs * CHIPS * BINS_DEV + UNROLL,), jnp.int32)] * 5


def spread_near(chip, meta, block, z_table):
    vmem = pl.BlockSpec(memory_space=pltpu.VMEM)
    return pl.pallas_call(
        near_kernel,
        out_shape=(
            pltpu.VMEM((2 * XS * DEPTH, LANES), jnp.float32),
            pltpu.VMEM((2, DEPTH, LANES), jnp.float32),
            pltpu.VMEM((8, LANES), jnp.int32),
        ),
        grid_spec=pltpu.PrefetchScalarGridSpec(
            num_scalar_prefetch=2,
            grid=(1,),
            in_specs=[vmem, pl.BlockSpec((None, NZ, 2 * LANES), lambda i, chip, meta: (chip[0], 0, 0))],
            out_specs=[vmem, vmem, vmem],
            scratch_shapes=bin_lists(1),
        ),
        compiler_params=pltpu.CompilerParams(vmem_limit_bytes=24 * 2**20),
        cost_estimate=pl.CostEstimate(flops=2**32, bytes_accessed=2**23, transcendentals=2**20),
        name="near",
    )(chip, meta, block, z_table)


def spread_far(core, metas, blocks, wave, load, grid):
    smem = pl.BlockSpec(memory_space=pltpu.SMEM)
    vmem = pl.BlockSpec(memory_space=pltpu.VMEM)
    return pl.pallas_call(
        far_kernel,
        out_shape=(
            pltpu.VMEM((XS * NY, LANES), jnp.bfloat16),
            pltpu.VMEM((XS * NY + 16, LANES), jnp.bfloat16),
            pltpu.VMEM((2 * XS * DEPTH, LANES), jnp.float32),
        ),
        in_specs=[smem] * 4 + [vmem] * 6,
        out_specs=[vmem] * 3,
        input_output_aliases={9: 2},
        scratch_shapes=[pltpu.VMEM(((SLABS - 1) * CHIPS * ROWS, LANES), jnp.int32)] + bin_lists(SLABS - 1),
        compiler_params=pltpu.CompilerParams(vmem_limit_bytes=24 * 2**20),
        name="far",
    )(core, *metas, *blocks, wave, load, grid)


def rows_kernel(home, own, other, load, table, out, helper_load):
    step = pl.program_id(0)

    @pl.when(step == 0)
    def _():
        theirs = other[XS * NY :, :].astype(jnp.float32)
        both = load[0:1, :].astype(jnp.float32) + theirs[0:1] * 256.0 + theirs[1:2]
        lane = lax.broadcasted_iota(jnp.int32, (1, LANES), 1)
        helper_load[0, 0] = jnp.sum(jnp.where(lane == home[0], both, 0.0)) * (1.0 / BIN)

    lines = []
    for x in range(PLANES):
        at = pl.ds(pl.multiple_of((step * PLANES + x) * NY, NY), NY)
        both = own[at, :].astype(jnp.float32) + other[at, :].astype(jnp.float32)
        lines.append(both.astype(jnp.bfloat16).T)
    lines = jnp.concatenate(lines, axis=0)
    width = NY // TILES
    for t in range(TILES):
        at = slice(t * width, (t + 1) * width)
        cos = jnp.dot(lines, table[0, :, at], preferred_element_type=jnp.float32)
        sin = jnp.dot(lines, table[1, :, at], preferred_element_type=jnp.float32)
        for x in range(PLANES):
            real = slice(x * LANES, x * LANES + 64)
            imag = slice(x * LANES + 64, (x + 1) * LANES)
            out[0, x, :, at] = cos[real] + sin[imag]
            out[1, x, :, at] = cos[imag] - sin[real]


def along_rows(home, own, other, load, y_table):
    smem = pl.BlockSpec(memory_space=pltpu.SMEM)
    vmem = pl.BlockSpec(memory_space=pltpu.VMEM)
    return pl.pallas_call(
        rows_kernel,
        out_shape=(
            jax.ShapeDtypeStruct((2, XS, 64, NY), jnp.float32),
            jax.ShapeDtypeStruct((1, 1), jnp.float32),
        ),
        grid=(XS // PLANES,),
        in_specs=[
            smem,
            vmem,
            vmem,
            vmem,
            vmem,
        ],
        out_specs=[pl.BlockSpec((2, PLANES, 64, NY), lambda i: (0, i, 0, 0)), smem],
        compiler_params=pltpu.CompilerParams(vmem_limit_bytes=24 * 2**20),
        name="rows",
    )(home, own, other, load, y_table)


def slab_shift(block, distance):
    count = lax.axis_size("wide")
    return lax.ppermute(block, "wide", [(i, (i + distance) % count) for i in range(count)])


def chip_shift(block, distance):
    count = lax.axis_size("narrow")
    return lax.ppermute(block, "narrow", [(i, (i + 2 * distance) % count) for i in range(count)])


def partner(block):
    count = lax.axis_size("narrow")
    return lax.ppermute(block, "narrow", [(i, i ^ 1) for i in range(count)])


def ring(block):
    near = jnp.concatenate([chip_shift(block, 1), block, chip_shift(block, -1)], axis=0)
    before = chip_shift(near, 3)
    after = chip_shift(near[: 2 * ROWS], -3)
    return jnp.concatenate([near, before, after], axis=0)


def metas_of(block):
    return block.reshape(CHIPS, ROWS, LANES)[:, META]


def body(positions, forces, counts, anchors, helpers):
    z_table, y_table = tables()
    z_table = pltpu.with_memory_space_constraint(jnp.asarray(z_table), pltpu.HBM)
    y_table = pltpu.with_memory_space_constraint(jnp.asarray(y_table), pltpu.VMEM)
    index = lax.axis_index("narrow").astype(jnp.int32)
    home, chip, core = index.reshape(1), (index >> 1).reshape(1), (index & 1).reshape(1)
    packed = pack(positions, forces, counts, anchors, helpers.reshape(BINS_DEV), home)
    block = ring(packed)
    blocks = [slab_shift(block, d) for d in range(1, SLABS)]
    grid, wave, load = spread_near(chip, metas_of(block), block, z_table)
    own, other, _ = spread_far(core, [metas_of(g) for g in blocks], blocks, wave, load, grid)
    arrived = pltpu.with_memory_space_constraint(partner(other), pltpu.VMEM)
    spectrum, helper_load = along_rows(home, own, arrived, load, y_table)
    return (spectrum, helper_load)


def solution(mesh):
    return jax.shard_map(
        body,
        mesh=mesh,
        in_specs=(
            P(("wide", "narrow"), None, None),
            P(("wide", "narrow"), None),
            P(("wide", "narrow")),
            P(None, ("wide", "narrow")),
            P(("wide", "narrow"), None),
        ),
        out_specs=(P(None, "wide", "narrow", None), P("wide", "narrow")),
        check_vma=False,
    )
```

time: 72.6 us -> 65.5 us (0.902); the launches traced: 71.5 us -> 66.2 us
  Pallas kernels: 30.4 us -> 26 us
  waiting for transfers between devices: 17.7 us -> 20 us
  between operations: 2.54 us -> 0.69 us
  other arithmetic: 2.45 us -> 1.51 us
    pallas_call x2, Pallas kernels: 23.2 us -> 17.3 us  [the longest x1 10.9 us: spread_far(): pl.pallas_call(far_kernel, out_shape=(pltpu.VMEM((XS * NY, LANES), jnp.bf...]
    ppermute x3, waiting for transfers between devices: 6.36 us -> 8.03 us  [slab_shift(): lax.ppermute(block, 'wide', [(i, (i + distance) % count) for i in range(c...]
    pallas_call x1, Pallas kernels: 5.62 us -> 7.14 us  [spread_near(): pl.pallas_call(near_kernel, out_shape=(pltpu.VMEM((2 * XS * DEPTH, LANES)...]
    reduce_sum x2 -> x0, other arithmetic: 0.77 us -> none  [the longest x1 0.67 us: body(): jnp.sum(jnp.where(helper_index == home, load, 0.0)) / BIN]
    ppermute x2 -> x1, waiting for transfers between devices: 3.15 us -> 3.79 us  [partner(): return lax.ppermute(block, 'narrow', [(i, i ^ 1) for i in range(count)])]
    ppermute x2 -> x1, starting transfers between devices: 2.88 us -> 2.58 us  [partner(): return lax.ppermute(block, 'narrow', [(i, i ^ 1) for i in range(count)])]
  transfers between devices with their start and end apart: 9 -> 8, of which waited for: 4 -> 5; matrix products, arithmetic and copies ran while one was open for 5% -> 3% of each run, Pallas kernels for 8% -> 11%
where the time goes in v3:
time: 65.5 us; the launch traced here: 66.2 us
  Pallas kernels  26 us (40%)
  waiting for transfers between devices  20 us (31%)
  starting transfers between devices  17.2 us (26%)
  other arithmetic  1.51 us (2%)
  local copies, waits for them, and re-layouts  0.79 us (1%)
  between operations  0.69 us (1%)
    pallas_call x1, Pallas kernels, spread_far(): pl.pallas_call(far_kernel, out_shape=(pltpu.VMEM((XS * NY, LANES), jnp.bf...  10.9 us
    ppermute x4, starting transfers between devices, chip_shift(): lax.ppermute(block, 'narrow', [(i, (i + 2 * distance) % count) for i in r...  9.94 us
    ppermute x4, waiting for transfers between devices, chip_shift(): lax.ppermute(block, 'narrow', [(i, (i + 2 * distance) % count) for i in r...  8.16 us
    ppermute x3, waiting for transfers between devices, slab_shift(): lax.ppermute(block, 'wide', [(i, (i + distance) % count) for i in range(c...  8.03 us
    pallas_call x1, Pallas kernels, spread_near(): pl.pallas_call(near_kernel, out_shape=(pltpu.VMEM((2 * XS * DEPTH, LANES)...  7.14 us
    pallas_call x1, Pallas kernels, along_rows(): pl.pallas_call(rows_kernel, out_shape=(jax.ShapeDtypeStruct((2, XS, 64, N...  6.39 us
    ppermute x3, starting transfers between devices, slab_shift(): lax.ppermute(block, 'wide', [(i, (i + distance) % count) for i in range(c...  4.69 us
    ppermute x1, waiting for transfers between devices, partner(): return lax.ppermute(block, 'narrow', [(i, i ^ 1) for i in range(count)])  3.79 us
  transfers between devices with their start and end apart: 8, of which 5 were waited for; matrix products, arithmetic and copies ran while one was open for 3% of the time, Pallas kernels for 11%

profile of v3, /device:TPU:1, one launch (start us, length us, event | category | flops | bytes accessed | tf_op | source)
XLA Modules:
  0.0 66.2 jit_solution(1572081632506876999)
XLA Ops:
  0.6 1.6 %pack.1 = s32[56,128]{1,0:T(8,128)} custom-call(s32[12]{0:T(128)} %counts.1, s32[3,12]{1,0:T(4,128)} %anchors.1, s32[12]{0:T(128)} %bitcast.28, s32[1]{0:T(128)} %bitcast.home, f32[12,3,256]{2,1,0:T(4,128)} %positions.1, f32[12,256]{1,0:T(8,128)} %forces.1), custom_call_target="tpu_custom_call" | custom-call | tf_op jit(solution)/shard_map/pack/pallas_call | solution.py:84
  2.2 2.5 %collective-permute-start = (s32[56,128]{1,0:T(8,128)}, s32[56,128]{1,0:T(8,128)S(1)}, u32[]{:S(2)}, u32[]{:S(2)}) collective-permute-start(s32[56,128]{1,0:T(8,128)} %pack.1), channel_id=1, source_target_pairs={{0,2},{1,3},{2,4},{3,5},{4,6},{5,7},{6,8},{7,9},{8,10},{9,11},{10,... | collective-permute-start | bytes 86024 | tf_op jit(solution)/shard_map/ppermute | solution.py:317
  4.7 3.9 %collective-permute-start.1 = (s32[56,128]{1,0:T(8,128)}, s32[56,128]{1,0:T(8,128)S(1)}, u32[]{:S(2)}, u32[]{:S(2)}) collective-permute-start(s32[56,128]{1,0:T(8,128)} %pack.1), channel_id=1, source_target_pairs={{0,14},{1,15},{2,0},{3,1},{4,2},{5,3},{6,4},{7,5},{8,6},{9,7},{10,... | collective-permute-start | bytes 86024 | tf_op jit(solution)/shard_map/ppermute | solution.py:317
  8.6 1.5 %collective-permute-done = s32[56,128]{1,0:T(8,128)S(1)} collective-permute-done((s32[56,128]{1,0:T(8,128)}, s32[56,128]{1,0:T(8,128)S(1)}, u32[]{:S(2)}, u32[]{:S(2)}) %collective-permute-start) | collective-permute-done | bytes 28704 | tf_op jit(solution)/shard_map/ppermute | solution.py:317
  10.1 0.8 %pad_add_fusion.1 = s32[112,128]{1,0:T(8,128)S(1)} fusion(s32[56,128]{1,0:T(8,128)} %pack.1, s32[56,128]{1,0:T(8,128)S(1)} %collective-permute-done), kind=kLoop, calls=%fused_computation.1 | loop fusion | flops 14336 | bytes 114688 | tf_op jit(solution)/shard_map/concatenate | solution.py:326
  10.8 2.4 %collective-permute-start.3 = (s32[112,128]{1,0:T(8,128)S(1)}, s32[112,128]{1,0:T(8,128)S(1)}, u32[]{:S(2)}, u32[]{:S(2)}) collective-permute-start(s32[112,128]{1,0:T(8,128)S(1)} %pad_add_fusion.1), channel_id=1, source_target_pairs={{0,10},{1,11},{2,12},{3,13},{4,14},{5,15},{6,0},{7,1},{8,2},{9,3},... | collective-permute-start | bytes 172040 | tf_op jit(solution)/shard_map/ppermute | solution.py:317
  13.2 0.0 collective-permute-done.1
  13.2 0.8 %pad_add_fusion = s32[168,128]{1,0:T(8,128)S(1)} fusion(s32[56,128]{1,0:T(8,128)S(1)} %collective-permute-done.1, s32[56,128]{1,0:T(8,128)} %pack.1, s32[56,128]{1,0:T(8,128)S(1)} %collective-permute-done), kind=kLoop, calls=%fused_computation | loop fusion | flops 43008 | bytes 172032 | tf_op jit(solution)/shard_map/concatenate | solution.py:326
  13.9 1.2 %collective-permute-start.2 = (s32[168,128]{1,0:T(8,128)S(1)}, s32[168,128]{1,0:T(8,128)S(1)}, u32[]{:S(2)}, u32[]{:S(2)}) collective-permute-start(s32[168,128]{1,0:T(8,128)S(1)} %pad_add_fusion), channel_id=1, source_target_pairs={{0,6},{1,7},{2,8},{3,9},{4,10},{5,11},{6,12},{7,13},{8,14},{9,15},... | collective-permute-start | bytes 258056 | tf_op jit(solution)/shard_map/ppermute | solution.py:317
  15.1 0.8 %constant_dynamic-update-slice_fusion.3 = s32[448,128]{1,0:T(8,128)S(1)} fusion(s32[448,128]{1,0:T(8,128)S(1)} %constant_dynamic-update-slice_fusion.4, s32[56,128]{1,0:T(8,128)} %pack.1), kind=kLoop, calls=%fused_computation.5 | loop fusion | bytes 57344
  15.9 6.7 %collective-permute-done.2 = s32[168,128]{1,0:T(8,128)S(1)} collective-permute-done((s32[168,128]{1,0:T(8,128)S(1)}, s32[168,128]{1,0:T(8,128)S(1)}, u32[]{:S(2)}, u32[]{:S(2)}) %collective-permute-start.2) | collective-permute-done | bytes 86048 | tf_op jit(solution)/shard_map/ppermute | solution.py:317
  22.6 0.0 collective-permute-done.3
  22.6 2.6 %collective-permute-start.6 = (s32[448,128]{1,0:T(8,128)S(1)}, s32[448,128]{1,0:T(8,128)S(1)}, u32[]{:S(2)}, u32[]{:S(2)}) collective-permute-start(s32[448,128]{1,0:T(8,128)S(1)} %constant_dynamic-update-slice_fusion.block), channel_id=1, source_target_pairs={{0,48},{16,64},{32,80},{48,96},{64,112},{80,128},{96,144},{112,160... | collective-permute-start | bytes 688136 | tf_op jit(solution)/shard_map/ppermute | solution.py:312
  25.2 1.5 %collective-permute-start.5 = (s32[448,128]{1,0:T(8,128)S(1)}, s32[448,128]{1,0:T(8,128)S(1)}, u32[]{:S(2)}, u32[]{:S(2)}) collective-permute-start(s32[448,128]{1,0:T(8,128)S(1)} %constant_dynamic-update-slice_fusion.block), channel_id=1, source_target_pairs={{0,32},{16,48},{32,64},{48,80},{64,96},{80,112},{96,128},{112,144}... | collective-permute-start | bytes 688136 | tf_op jit(solution)/shard_map/ppermute | solution.py:312
  26.7 0.6 collective-permute-start.4
  27.3 7.1 %near.1 = (f32[16768,128]{1,0:T(8,128)S(1)}, f32[2,1048,128]{2,1,0:T(8,128)S(1)}, s32[8,128]{1,0:T(8,128)S(1)}) custom-call(s32[1]{0:T(128)} %bitcast.9.chip, s32[8,128]{1,0:T(8,128)S(1)} %bitcast.27, s32[448,128]{1,0:T(8,128)S(1)} %constant_dynamic-update-slice_fusion.block, bf16[8,1024,256]{2,1,0:T(8,128)(2,1)} %constant.10.clone.table), custom_call_target="tpu_custom_call" | custom-call | flops 4294967296 | bytes 8388608 | tf_op jit(solution)/shard_map/near/pallas_call | solution.py:220
  34.5 0.0 collective-permute-done.6.g3
  34.5 0.5 collective-permute-done.5.g2
  35.0 7.5 %collective-permute-done.4.g1 = s32[448,128]{1,0:T(8,128)S(1)} collective-permute-done((s32[448,128]{1,0:T(8,128)S(1)}, s32[448,128]{1,0:T(8,128)S(1)}, u32[]{:S(2)}, u32[]{:S(2)}) %collective-permute-start.4) | collective-permute-done | bytes 229408 | tf_op jit(solution)/shard_map/ppermute | solution.py:312
  42.5 10.9 %far.1 = (bf16[8192,128]{1,0:T(8,128)(2,1)S(1)}, bf16[8208,128]{1,0:T(8,128)(2,1)S(1)}, f32[16768,128]{1,0:T(8,128)S(1)}) custom-call(s32[1]{0:T(128)} %bitcast.1.core, s32[8,128]{1,0:T(8,128)S(1)} %bitcast.25, s32[8,128]{1,0:T(8,128)S(1)} %bitcast.24, s32[8,128]{1,0:T(8,128)S(1)} %bitcast.23, ...), custom_call_target="tpu_custom_call", output_to_operand_aliasing={{2}: (9, {})} | custom-call | tf_op jit(solution)/shard_map/far/pallas_call | solution.py:243
  53.5 2.6 %collective-permute-start.7 = (bf16[8208,128]{1,0:T(8,128)(2,1)S(1)}, bf16[8208,128]{1,0:T(8,128)(2,1)S(1)}, u32[]{:S(2)}, u32[]{:S(2)}) collective-permute-start(bf16[8208,128]{1,0:T(8,128)(2,1)S(1)} %get-tuple-element.11), channel_id=1, source_target_pairs={{0,1},{1,0},{2,3},{3,2},{4,5},{5,4},{6,7},{7,6},{8,9},{9,8},{10,11... | collective-permute-start | bytes 6303752 | tf_op jit(solution)/shard_map/ppermute | solution.py:322
  56.0 3.8 %collective-permute-done.7.other = bf16[8208,128]{1,0:T(8,128)(2,1)S(1)} collective-permute-done((bf16[8208,128]{1,0:T(8,128)(2,1)S(1)}, bf16[8208,128]{1,0:T(8,128)(2,1)S(1)}, u32[]{:S(2)}, u32[]{:S(2)}) %collective-permute-start.7) | collective-permute-done | bytes 2101280 | tf_op jit(solution)/shard_map/ppermute | solution.py:322
  59.8 0.0 copy-done
  59.8 6.4 %rows.1 = (f32[2,8,64,1024]{3,2,1,0:T(8,128)}, f32[1,1]{1,0:T(1,128)}) custom-call(s32[1]{0:T(128)} %bitcast.home, bf16[8192,128]{1,0:T(8,128)(2,1)S(1)} %get-tuple-element.10.own, bf16[8208,128]{1,0:T(8,128)(2,1)S(1)} %collective-permute-done.7.other, s32[8,128]{1,0:T(8,128)S(1)} %get-tuple-element.8.load, bf16[2,1024,1024]{2,1,0:T(8,128)(2,1)S(1)} %copy-done), custom_call_target="tpu_custom_call" | custom-call | tf_op jit(solution)/shard_map/rows/pallas_call | solution.py:290
  (9 shorter events, 0.0 us)
Async XLA Ops:
  2.2 7.9 %collective-permute-start = (s32[56,128]{1,0:T(8,128)}, s32[56,128]{1,0:T(8,128)S(1)}, u32[]{:S(2)}, u32[]{:S(2)}) collective-permute-start(s32[56,128]{1,0:T(8,128)} %pack.1), channel_id=1, source_target_pairs={{0,2},{1,3},{2,4},{3,5},{4,6},{5,7},{6,8},{7,9},{8,10},{9,11},{10,... | collective-permute-start | bytes 86024 | tf_op jit(solution)/shard_map/ppermute | solution.py:317
  4.7 8.5 %collective-permute-start.1 = (s32[56,128]{1,0:T(8,128)}, s32[56,128]{1,0:T(8,128)S(1)}, u32[]{:S(2)}, u32[]{:S(2)}) collective-permute-start(s32[56,128]{1,0:T(8,128)} %pack.1), channel_id=1, source_target_pairs={{0,14},{1,15},{2,0},{3,1},{4,2},{5,3},{6,4},{7,5},{8,6},{9,7},{10,... | collective-permute-start | bytes 86024 | tf_op jit(solution)/shard_map/ppermute | solution.py:317
  10.8 11.8 %collective-permute-start.3 = (s32[112,128]{1,0:T(8,128)S(1)}, s32[112,128]{1,0:T(8,128)S(1)}, u32[]{:S(2)}, u32[]{:S(2)}) collective-permute-start(s32[112,128]{1,0:T(8,128)S(1)} %pad_add_fusion.1), channel_id=1, source_target_pairs={{0,10},{1,11},{2,12},{3,13},{4,14},{5,15},{6,0},{7,1},{8,2},{9,3},... | collective-permute-start | bytes 172040 | tf_op jit(solution)/shard_map/ppermute | solution.py:317
  13.9 8.6 %collective-permute-start.2 = (s32[168,128]{1,0:T(8,128)S(1)}, s32[168,128]{1,0:T(8,128)S(1)}, u32[]{:S(2)}, u32[]{:S(2)}) collective-permute-start(s32[168,128]{1,0:T(8,128)S(1)} %pad_add_fusion), channel_id=1, source_target_pairs={{0,6},{1,7},{2,8},{3,9},{4,10},{5,11},{6,12},{7,13},{8,14},{9,15},... | collective-permute-start | bytes 258056 | tf_op jit(solution)/shard_map/ppermute | solution.py:317
  22.6 11.9 %collective-permute-start.6 = (s32[448,128]{1,0:T(8,128)S(1)}, s32[448,128]{1,0:T(8,128)S(1)}, u32[]{:S(2)}, u32[]{:S(2)}) collective-permute-start(s32[448,128]{1,0:T(8,128)S(1)} %constant_dynamic-update-slice_fusion.block), channel_id=1, source_target_pairs={{0,48},{16,64},{32,80},{48,96},{64,112},{80,128},{96,144},{112,160... | collective-permute-start | bytes 688136 | tf_op jit(solution)/shard_map/ppermute | solution.py:312
  25.2 9.9 %collective-permute-start.5 = (s32[448,128]{1,0:T(8,128)S(1)}, s32[448,128]{1,0:T(8,128)S(1)}, u32[]{:S(2)}, u32[]{:S(2)}) collective-permute-start(s32[448,128]{1,0:T(8,128)S(1)} %constant_dynamic-update-slice_fusion.block), channel_id=1, source_target_pairs={{0,32},{16,48},{32,64},{48,80},{64,96},{80,112},{96,128},{112,144}... | collective-permute-start | bytes 688136 | tf_op jit(solution)/shard_map/ppermute | solution.py:312
  26.7 15.8 %collective-permute-start.4 = (s32[448,128]{1,0:T(8,128)S(1)}, s32[448,128]{1,0:T(8,128)S(1)}, u32[]{:S(2)}, u32[]{:S(2)}) collective-permute-start(s32[448,128]{1,0:T(8,128)S(1)} %constant_dynamic-update-slice_fusion.block), channel_id=1, source_target_pairs={{0,16},{16,32},{32,48},{48,64},{64,80},{80,96},{96,112},{112,128},... | collective-permute-start | bytes 688136 | tf_op jit(solution)/shard_map/ppermute | solution.py:312
  42.5 17.3 %copy-start = (bf16[2,1024,1024]{2,1,0:T(8,128)(2,1)S(1)}, bf16[2,1024,1024]{2,1,0:T(8,128)(2,1)}, u32[]{:S(2)}) copy-start(bf16[2,1024,1024]{2,1,0:T(8,128)(2,1)} %constant.11.clone.table) | copy-start | bytes 12582916
  53.5 6.4 %collective-permute-start.7 = (bf16[8208,128]{1,0:T(8,128)(2,1)S(1)}, bf16[8208,128]{1,0:T(8,128)(2,1)S(1)}, u32[]{:S(2)}, u32[]{:S(2)}) collective-permute-start(bf16[8208,128]{1,0:T(8,128)(2,1)S(1)} %get-tuple-element.11), channel_id=1, source_target_pairs={{0,1},{1,0},{2,3},{3,2},{4,5},{5,4},{6,7},{7,6},{8,9},{9,8},{10,11... | collective-permute-start | bytes 6303752 | tf_op jit(solution)/shard_map/ppermute | solution.py:322
